TPU v7x, 32 devices: a whole 2x2x4 slice. The times are simulated.
32 devices in a mesh: groups: 2 (over y), tiles: 4 (over z), chan: 2 (over x), sub: 2 (over core).
Axes of the slice: x: 2, y: 2, z: 4, core: 2. Of those that a mesh axis runs over, the one named last changes fastest.
Arguments:
- features: bfloat16 [128, 256, 256], P(('groups', 'tiles', 'sub'), 'chan'), parts along dimension 0, may hold values from -6 to 6
- cotangent: bfloat16 [128, 256, 256], P(('groups', 'tiles', 'sub'), 'chan'), parts along dimension 0, may hold values from -6 to 6
- down_factor: bfloat16 [2, 256, 64], P(None, 'chan'), may hold values from -0.375 to 0.375
- core_kernel: bfloat16 [2, 9, 64, 64], replicated, may hold values from -0.25 to 0.25
- up_factor: bfloat16 [2, 256, 64], P(None, 'chan'), may hold values from -0.75 to 0.75
- tile_count: int32 [16], P(('groups', 'tiles', 'sub')), parts along dimension 0, may hold values from 4 to 8, as said below
- neighbour_owner: int32 [128, 8], P(('groups', 'tiles', 'sub')), parts along dimension 0, may hold values from -1 to 7, as said below
- neighbour_slot: int32 [128, 8], P(('groups', 'tiles', 'sub')), parts along dimension 0, may hold values from -1 to 7, as said below
Outputs:
- input_gradient: bfloat16 [128, 256, 256], P(('groups', 'tiles', 'sub'), 'chan'), parts along dimension 0
- down_gradient: float32 [4, 256, 64], P('groups', 'chan'), parts along dimension 0
- core_gradient: float32 [4, 9, 64, 64], P('groups', None, 'chan'), parts along dimension 0
- up_gradient: float32 [4, 256, 64], P('groups', 'chan'), parts along dimension 0
There are 2 independent parts, one for each index of `groups`. A program takes and returns all parts, laid end to end along the dimension named above; an argument that names none is the same for every part. Nothing has to cross between parts.
Inputs may be any that keep to these rules, and one draw needn't show every extreme that they name: `tile_count`: every count is even; some device holds exactly 8 live tiles and some exactly 4. `neighbour_owner`: -1 where the slot is not live or no tissue tile lies in that direction. Otherwise the owner is the slot's own device or the device just before or after it along the owners, and the named slot is live there. Neighbourhood is mutual: if tile h lies in some direction of tile g, then g lies in the opposite direction of h. `neighbour_slot`: -1 exactly where neighbour_owner is -1.
All inputs are finite; a program needn't handle non-finite values.
Results may differ from a plain program's by a relative error of at most 0.014.
Values may be sent and summed in bfloat16 or wider, within the bound.
A program may use at most 64 MiB of HBM per device.

v0:
```python
import jax
import jax.numpy as jnp
from jax import lax
from jax.sharding import PartitionSpec as P

TILE = 16
LAYERS = 2


EDGE_ROWS = [1, 6, 3, 4]
EDGE_PIECES = [1, 0, 3, 2]
CORNER_ROWS = [0, 2, 5, 7]
CORNER_PIECES = [3, 2, 1, 0]


def padded_2(cells, sides, width):
    for axis, dim in sides:
        count = lax.axis_size(axis)
        ends = count - 1
        head = lax.slice_in_dim(cells, 0, width, axis=dim)
        tail = lax.slice_in_dim(cells, cells.shape[dim] - width, cells.shape[dim], axis=dim)
        cells = jnp.concatenate(
            [
                lax.ppermute(tail, axis, [(i, (i + 1) % count) for i in range(ends)]),
                cells,
                lax.ppermute(head, axis, [((i + 1) % count, i) for i in range(ends)]),
            ],
            axis=dim,
        )
    return cells


def cycle_of(squares):
    edge_cells = jnp.concatenate(
        [squares[:, :, 0, :], squares[:, :, -1, :], squares[:, :, :, 0], squares[:, :, :, -1]],
        axis=2,
    )
    corners = jnp.stack(
        [squares[:, :, 0, 0], squares[:, :, 0, -1], squares[:, :, -1, 0], squares[:, :, -1, -1]],
        axis=2,
    )
    return jnp.concatenate([edge_cells, corners], axis=2)


def assemble(squares, side_cells, corner_cells):
    top_row = jnp.concatenate(
        [corner_cells[0][:, :, None], side_cells[0], corner_cells[1][:, :, None]], axis=2
    )
    bottom_row = jnp.concatenate(
        [corner_cells[2][:, :, None], side_cells[1], corner_cells[3][:, :, None]], axis=2
    )
    middle = jnp.concatenate(
        [side_cells[2][:, :, :, None], squares, side_cells[3][:, :, :, None]], axis=3
    )
    return jnp.concatenate([top_row[:, :, None, :], middle, bottom_row[:, :, None, :]], axis=2)


def selectors(neighbour_owner, neighbour_slot, device_here, slot_total):
    local_row = (neighbour_owner - device_here + 1) * slot_total + neighbour_slot
    columns = jnp.arange(3 * slot_total)
    matched = (local_row[:, :, None] == columns[None, None, :]) & (neighbour_owner[:, :, None] >= 0)
    return matched.astype(jnp.bfloat16)


def place_border(flat_cells, extended, chooser):
    squares = flat_cells.reshape(flat_cells.shape[0], flat_cells.shape[1], TILE, TILE)
    nearest = jnp.einsum(
        "uvd,dck->uvck",
        chooser[:, EDGE_ROWS, :],
        extended[:, :, : 4 * TILE],
        preferred_element_type=jnp.float32,
    ).astype(jnp.bfloat16)
    diagonal = jnp.einsum(
        "uvd,dck->uvck",
        chooser[:, CORNER_ROWS, :],
        extended[:, :, 4 * TILE :],
        preferred_element_type=jnp.float32,
    ).astype(jnp.bfloat16)
    side_cells = [
        nearest[:, which_side, :, piece_index * TILE : (piece_index + 1) * TILE]
        for which_side, piece_index in enumerate(EDGE_PIECES)
    ]
    corner_cells = [
        diagonal[:, which_side, :, piece_index]
        for which_side, piece_index in enumerate(CORNER_PIECES)
    ]
    return assemble(squares, side_cells, corner_cells)


def window(padded, shift_rows, shift_cols):
    section = padded[:, :, shift_rows : shift_rows + TILE, shift_cols : shift_cols + TILE]
    return section.reshape(section.shape[0], section.shape[1], TILE * TILE)


def stacked_windows(padded, flipped):
    if flipped:
        return jnp.stack(
            [window(padded, 2 - offset // 3, 2 - offset % 3) for offset in range(9)], axis=0
        )
    return jnp.stack([window(padded, offset // 3, offset % 3) for offset in range(9)], axis=0)


def forward_conv(windows, kernel):
    return jnp.einsum("tsr,turq->usq", kernel, windows, preferred_element_type=jnp.float32)


def backward_conv(padded, kernel):
    return jnp.einsum(
        "tsr,tusq->urq", kernel, stacked_windows(padded, True), preferred_element_type=jnp.float32
    )


def core_gradient_of(gradient, windows):
    return jnp.einsum("usq,turq->tsr", gradient, windows, preferred_element_type=jnp.float32)


def blocked_product(factor, data, members):
    width = factor.shape[0] // members
    running = jnp.zeros((data.shape[0], factor.shape[1], data.shape[2]), jnp.float32)
    for member in range(members):
        partial_value = jnp.einsum(
            "cr,ucq->urq",
            factor[member * width : (member + 1) * width],
            data[:, member * width : (member + 1) * width],
            preferred_element_type=jnp.float32,
        )
        running = running + lax.optimization_barrier(partial_value.astype(jnp.bfloat16)).astype(
            jnp.float32
        )
    return running.astype(jnp.bfloat16)


def settle(down_part, core_part, up_part):
    return (down_part, core_part, up_part)


def whole_tiles(
    features,
    cotangent,
    down_factor,
    core_kernel,
    up_factor,
    tile_count,
    neighbour_owner,
    neighbour_slot,
):
    slot_total = features.shape[0]
    members = lax.axis_size("chan")
    rows_here = slot_total // members
    device_here = lax.axis_index(("tiles", "sub"))
    first_slot = lax.axis_index("chan") * rows_here
    hidden, upstream = (
        lax.all_to_all(features, "chan", split_axis=0, concat_axis=1, tiled=True),
        lax.all_to_all(cotangent, "chan", split_axis=0, concat_axis=1, tiled=True),
    )
    alive = (first_slot + jnp.arange(rows_here) < tile_count[0]).astype(jnp.bfloat16)
    hidden = hidden * alive[:, None, None]
    upstream = upstream * alive[:, None, None]
    down_whole, up_whole = (
        lax.all_gather(down_factor, "chan", axis=1, tiled=True),
        lax.all_gather(up_factor, "chan", axis=1, tiled=True),
    )
    near_owner = lax.dynamic_slice_in_dim(neighbour_owner, first_slot, rows_here, 0)
    near_slot = lax.dynamic_slice_in_dim(neighbour_slot, first_slot, rows_here, 0)
    chooser = selectors(near_owner, near_slot, device_here, slot_total)

    def padded_of(cells):
        border = cycle_of(cells.reshape(rows_here, cells.shape[1], TILE, TILE))
        owner_cycle = lax.all_gather(border, "chan", axis=0, tiled=True)
        extended = padded_2(owner_cycle, ((("tiles", "sub"), 0),), slot_total)
        return place_border(cells, extended, chooser)

    saved_layers = []
    for layer_index in range(LAYERS):
        activations = blocked_product(down_whole[layer_index], hidden, members)
        windows = stacked_windows(padded_of(activations), False)
        mixed = forward_conv(windows, core_kernel[layer_index]).astype(jnp.bfloat16)
        preact = jnp.einsum(
            "cs,usq->ucq", up_whole[layer_index], mixed, preferred_element_type=jnp.float32
        )
        saved_layers.append((hidden, windows, mixed, preact))
        hidden = (hidden.astype(jnp.float32) + jax.nn.silu(preact)).astype(jnp.bfloat16)
    down_list = [None] * LAYERS
    core_list = [None] * LAYERS
    up_list = [None] * LAYERS
    for layer_index in reversed(range(LAYERS)):
        hidden, windows, mixed, preact = saved_layers[layer_index]
        squashed = jax.nn.sigmoid(preact)
        pre_gradient = (
            upstream.astype(jnp.float32) * squashed * (1.0 + preact * (1.0 - squashed))
        ).astype(jnp.bfloat16)
        up_part = jnp.einsum("ucq,usq->cs", pre_gradient, mixed, preferred_element_type=jnp.float32)
        mixed_gradient = blocked_product(up_whole[layer_index], pre_gradient, members)
        core_part = core_gradient_of(mixed_gradient, windows)
        gradient_padded = padded_of(mixed_gradient)
        act_gradient = backward_conv(gradient_padded, core_kernel[layer_index]).astype(jnp.bfloat16)
        down_part = jnp.einsum(
            "ucq,urq->cr", hidden, act_gradient, preferred_element_type=jnp.float32
        )
        through = jnp.einsum(
            "cr,urq->ucq", down_whole[layer_index], act_gradient, preferred_element_type=jnp.float32
        )
        upstream = (upstream.astype(jnp.float32) + through).astype(jnp.bfloat16)
        down_part, up_part = (
            lax.psum_scatter(
                down_part.astype(jnp.bfloat16), "chan", scatter_dimension=0, tiled=True
            ).astype(jnp.float32),
            lax.psum_scatter(
                up_part.astype(jnp.bfloat16), "chan", scatter_dimension=0, tiled=True
            ).astype(jnp.float32),
        )
        core_part = lax.psum_scatter(
            core_part.astype(jnp.bfloat16), "chan", scatter_dimension=1, tiled=True
        ).astype(jnp.float32)
        down_list[layer_index], core_list[layer_index], up_list[layer_index] = settle(
            down_part, core_part, up_part
        )
    upstream = lax.all_to_all(upstream, "chan", split_axis=1, concat_axis=0, tiled=True)
    return (upstream, down_list, core_list, up_list)


def local(
    features,
    cotangent,
    down_factor,
    core_kernel,
    up_factor,
    tile_count,
    neighbour_owner,
    neighbour_slot,
):
    upstream, down_list, core_list, up_list = whole_tiles(
        features,
        cotangent,
        down_factor,
        core_kernel,
        up_factor,
        tile_count,
        neighbour_owner,
        neighbour_slot,
    )
    down_gradient = jnp.stack(down_list, axis=0)
    core_gradient = jnp.stack(core_list, axis=0)
    up_gradient = jnp.stack(up_list, axis=0)
    down_gradient, core_gradient, up_gradient = lax.psum(
        (down_gradient, core_gradient, up_gradient), ("tiles", "sub")
    )
    return (upstream, down_gradient, core_gradient, up_gradient)


def solution(mesh):
    return jax.shard_map(
        local,
        mesh=mesh,
        in_specs=(
            P(("groups", "tiles", "sub"), "chan", None),
            P(("groups", "tiles", "sub"), "chan", None),
            P(None, "chan", None),
            P(),
            P(None, "chan", None),
            P(("groups", "tiles", "sub")),
            P(("groups", "tiles", "sub"), None),
            P(("groups", "tiles", "sub"), None),
        ),
        out_specs=(
            P(("groups", "tiles", "sub"), "chan", None),
            P("groups", "chan", None),
            P("groups", None, "chan", None),
            P("groups", "chan", None),
        ),
        check_vma=False,
    )
```

profile of v0, /device:TPU:0, one launch (start us, length us, event | category | flops | bytes accessed | tf_op | source)
XLA Modules:
  0.0 312.5 jit_solution(5024277569459636531)
XLA Ops:
  7.2 4.2 %all-to-all-start.1 = ((bf16[8,128,256]{2,1,0:T(8,128)(2,1)}), bf16[8,128,256]{2,1,0:T(8,128)(2,1)S(1)}, u32[]{:S(2)}, u32[]{:S(2)}) async-start(bf16[8,128,256]{2,1,0:T(8,128)(2,1)} %param.16), calls=%async_computation.1 | async-start | bytes 1048576 | tf_op jit(solution)/shard_map/all_to_all | solution.py:153
  13.5 6.7 %all-to-all-done.1 = bf16[8,128,256]{2,1,0:T(8,128)(2,1)S(1)} async-done(((bf16[8,128,256]{2,1,0:T(8,128)(2,1)}), bf16[8,128,256]{2,1,0:T(8,128)(2,1)S(1)}, u32[]{:S(2)}, u32[]{:S(2)}) %all-to-all-start.1) | async-done | bytes 524320 | tf_op jit(solution)/shard_map/all_to_all | solution.py:153
  20.1 3.5 %all-to-all-start = ((bf16[8,128,256]{2,1,0:T(8,128)(2,1)}), bf16[8,128,256]{2,1,0:T(8,128)(2,1)S(1)}, u32[]{:S(2)}, u32[]{:S(2)}) async-start(bf16[8,128,256]{2,1,0:T(8,128)(2,1)} %param.17), calls=%async_computation | async-start | bytes 1048576 | tf_op jit(solution)/shard_map/all_to_all | solution.py:154
  23.9 8.2 %all_gather.18 = bf16[2,256,64]{1,2,0:T(8,128)(2,1)S(1)} all-gather(bf16[2,128,64]{1,2,0:T(8,128)(2,1)S(1)} %copy-done.42), channel_id=1, replica_groups=mesh['groups'=2,'tiles'=4,'chan'=2,'sub'=2] {'chan'}, dimensions={1}, use_global_device_ids=true | all-gather | bytes 98304 | tf_op jit(solution)/shard_map/all_gather | solution.py:160
  34.1 4.9 %all_gather.19 = bf16[8,64,68]{2,1,0:T(8,128)(2,1)S(1)} all-gather(bf16[4,64,68]{2,1,0:T(8,128)(2,1)S(1)} %copy.710), channel_id=1, replica_groups=mesh['groups'=2,'tiles'=4,'chan'=2,'sub'=2] {'chan'}, dimensions={0}, use_global_device_ids=true | all-gather | bytes 104448 | tf_op jit(solution)/shard_map/all_gather | solution.py:169
  40.5 3.0 collective-permute-start
  44.7 4.8 %all_gather.20 = bf16[2,256,64]{1,2,0:T(8,128)(2,1)S(1)} all-gather(bf16[2,128,64]{1,2,0:T(8,128)(2,1)S(1)} %copy-done.43), channel_id=1, replica_groups=mesh['groups'=2,'tiles'=4,'chan'=2,'sub'=2] {'chan'}, dimensions={1}, use_global_device_ids=true | all-gather | bytes 98304 | tf_op jit(solution)/shard_map/all_gather | solution.py:161
  57.8 4.9 %all_gather.21 = bf16[8,64,68]{2,1,0:T(8,128)(2,1)S(1)} all-gather(bf16[4,64,68]{2,1,0:T(8,128)(2,1)S(1)} %copy.744), channel_id=1, replica_groups=mesh['groups'=2,'tiles'=4,'chan'=2,'sub'=2] {'chan'}, dimensions={0}, use_global_device_ids=true | all-gather | bytes 104448 | tf_op jit(solution)/shard_map/all_gather | solution.py:169
  64.2 3.0 collective-permute-start.2
  90.2 5.1 %all_gather.22 = bf16[8,64,68]{2,1,0:T(8,128)(2,1)S(1)} all-gather(bf16[4,64,68]{2,1,0:T(8,128)(2,1)} %copy.778), channel_id=1, replica_groups=mesh['groups'=2,'tiles'=4,'chan'=2,'sub'=2] {'chan'}, dimensions={0}, use_global_device_ids=true | all-gather | bytes 104448 | tf_op jit(solution)/shard_map/all_gather | solution.py:169
  96.1 3.7 %collective-permute-start.4 = (bf16[8,64,68]{2,0,1:T(8,128)(2,1)}, bf16[8,64,68]{2,0,1:T(8,128)(2,1)}, u32[]{:S(2)}, u32[]{:S(2)}) collective-permute-start(bf16[8,64,68]{2,0,1:T(8,128)(2,1)} %copy.779), channel_id=1, source_target_pairs={{0,1},{1,4},{4,5},{5,8},{8,9},{9,12},{12,13},{2,3},{3,6},{6,7},{7,... | collective-permute-start | bytes 208904 | tf_op jit(solution)/shard_map/ppermute | solution.py:24
  99.8 1.9 fusion.27
  105.6 2.0 collective-permute-done.5
  108.8 1.9 copy.788
  118.9 1.7 pad_maximum_fusion.10
  127.1 1.7 copy.804
  130.6 1.7 copy.802
  133.3 1.8 copy.799
  135.1 1.7 copy.798
  136.8 1.8 copy.797
  148.1 5.1 %all_gather.23 = bf16[8,64,68]{2,1,0:T(8,128)(2,1)S(1)} all-gather(bf16[4,64,68]{2,1,0:T(8,128)(2,1)} %copy.813), channel_id=1, replica_groups=mesh['groups'=2,'tiles'=4,'chan'=2,'sub'=2] {'chan'}, dimensions={0}, use_global_device_ids=true | all-gather | bytes 104448 | tf_op jit(solution)/shard_map/all_gather | solution.py:169
  154.0 5.0 %collective-permute-start.6 = (bf16[8,64,68]{2,0,1:T(8,128)(2,1)}, bf16[8,64,68]{2,0,1:T(8,128)(2,1)}, u32[]{:S(2)}, u32[]{:S(2)}) collective-permute-start(bf16[8,64,68]{2,0,1:T(8,128)(2,1)} %copy.814), channel_id=1, source_target_pairs={{0,1},{1,4},{4,5},{5,8},{8,9},{9,12},{12,13},{2,3},{3,6},{6,7},{7,... | collective-permute-start | bytes 208904 | tf_op jit(solution)/shard_map/ppermute | solution.py:24
  159.0 2.0 fusion.25
  167.0 1.9 copy.823
  191.4 1.8 copy.834
  194.9 1.8 copy.832
  208.9 3.5 %all-to-all-start.2 = ((bf16[4,256,256]{2,0,1:T(4,128)(2,1)}), bf16[4,256,256]{2,0,1:T(4,128)(2,1)S(1)}, u32[]{:S(2)}, u32[]{:S(2)}) async-start(bf16[4,256,256]{2,0,1:T(4,128)(2,1)} %copy.842), calls=%async_computation.2 | async-start | bytes 1048576 | tf_op jit(solution)/shard_map/all_to_all | solution.py:218
  214.6 12.9 %reduce-scatter.17.cloned.1.call-done = bf16[9,32,64]{2,0,1:T(8,128)(2,1)} async-done(((bf16[9,64,64]{2,0,1:T(8,128)(2,1)}), bf16[9,32,64]{2,0,1:T(8,128)(2,1)}) %reduce-scatter.17.cloned.1.call-update) | async-done | bytes 36880 | tf_op jit(solution)/shard_map/reduce_scatter | solution.py:212
  227.5 13.8 %reduce-scatter.15.cloned.1.call-done = bf16[9,32,64]{2,0,1:T(8,128)(2,1)} async-done(((bf16[9,64,64]{2,0,1:T(8,128)(2,1)}), bf16[9,32,64]{2,0,1:T(8,128)(2,1)}) %reduce-scatter.15.cloned.1.call-update) | async-done | bytes 36880 | tf_op jit(solution)/shard_map/reduce_scatter | solution.py:212
  241.3 1.8 maximum_convert_fusion
  243.2 58.5 %all-reduce.3.cloned.1.call-done = (f32[2,128,64]{1,2,0:T(8,128)}, f32[2,9,32,64]{3,1,2,0:T(8,128)}, f32[2,128,64]{1,2,0:T(8,128)}) async-done(((f32[2,128,64]{1,2,0:T(8,128)}, f32[2,9,32,64]{3,1,2,0:T(8,128)}, f32[2,128,64]{1,2,0:T(8,128)}), (f32[2,128,64]{1,2,0:T(8,128)}, f32[2,9,32,64]{3,1,2,0:T(8,128)}, f32[2,128,64]{1,2,0:T(8,128)})) %all-reduce.3.cloned.1.call-update) | async-done | bytes 278544 | tf_op jit(solution)/shard_map/psum | solution.py:245
  301.7 1.9 copy.846
  (348 shorter events, 117.9 us)
Async XLA Ops:
  7.2 16.7 %copy-start.42 = (bf16[2,128,64]{1,2,0:T(8,128)(2,1)S(1)}, bf16[2,128,64]{1,2,0:T(8,128)(2,1)}, u32[]{:S(2)}) copy-start(bf16[2,128,64]{1,2,0:T(8,128)(2,1)} %param.18) | copy-start | bytes 98308
  7.2 12.9 %all-to-all-start.1 = ((bf16[8,128,256]{2,1,0:T(8,128)(2,1)}), bf16[8,128,256]{2,1,0:T(8,128)(2,1)S(1)}, u32[]{:S(2)}, u32[]{:S(2)}) async-start(bf16[8,128,256]{2,1,0:T(8,128)(2,1)} %param.16), calls=%async_computation.1 | async-start | bytes 1048576 | tf_op jit(solution)/shard_map/all_to_all | solution.py:153
  20.1 12.0 %all-to-all-start = ((bf16[8,128,256]{2,1,0:T(8,128)(2,1)}), bf16[8,128,256]{2,1,0:T(8,128)(2,1)S(1)}, u32[]{:S(2)}, u32[]{:S(2)}) async-start(bf16[8,128,256]{2,1,0:T(8,128)(2,1)} %param.17), calls=%async_computation | async-start | bytes 1048576 | tf_op jit(solution)/shard_map/all_to_all | solution.py:154
  23.6 179.0 %reduce-scatter.25.cloned.1.call-start = ((), (), s32[]{:S(2)}) async-start(), calls=%async_computation.14 | async-start | bytes 98304
  32.0 24.6 %copy-start.26 = (bf16[2,256,64]{1,2,0:T(8,128)(2,1)}, bf16[2,256,64]{1,2,0:T(8,128)(2,1)S(1)}, u32[]{:S(2)}) copy-start(bf16[2,256,64]{1,2,0:T(8,128)(2,1)S(1)} %all_gather.18) | copy-start | bytes 196612
  33.3 10.2 %copy-start.44 = (s32[4]{0:T(128)S(1)}, s32[4]{0:T(128)}, u32[]{:S(2)}) copy-start(s32[4]{0:T(128)} %constant.49) | copy-start | bytes 52
  33.3 10.2 %copy-start.45 = (s32[4]{0:T(128)S(1)}, s32[4]{0:T(128)}, u32[]{:S(2)}) copy-start(s32[4]{0:T(128)} %constant.48) | copy-start | bytes 52
  33.4 11.4 %copy-start.43 = (bf16[2,128,64]{1,2,0:T(8,128)(2,1)S(1)}, bf16[2,128,64]{1,2,0:T(8,128)(2,1)}, u32[]{:S(2)}) copy-start(bf16[2,128,64]{1,2,0:T(8,128)(2,1)} %param.20) | copy-start | bytes 98308
  39.2 10.3 %collective-permute-start.1 = (bf16[8,64,68]{1,0,2:T(8,128)(2,1)S(1)}, bf16[8,64,68]{1,0,2:T(8,128)(2,1)S(1)}, u32[]{:S(2)}, u32[]{:S(2)}) collective-permute-start(bf16[8,64,68]{1,0,2:T(8,128)(2,1)S(1)} %copy.711), channel_id=1, source_target_pairs={{1,0},{4,1},{5,4},{8,5},{9,8},{12,9},{13,12},{3,2},{6,3},{7,6},{10... | collective-permute-start | bytes 208904 | tf_op jit(solution)/shard_map/ppermute | solution.py:26
  40.5 9.1 %collective-permute-start = (bf16[8,64,68]{1,0,2:T(8,128)(2,1)S(1)}, bf16[8,64,68]{1,0,2:T(8,128)(2,1)S(1)}, u32[]{:S(2)}, u32[]{:S(2)}) collective-permute-start(bf16[8,64,68]{1,0,2:T(8,128)(2,1)S(1)} %copy.711), channel_id=1, source_target_pairs={{0,1},{1,4},{4,5},{5,8},{8,9},{9,12},{12,13},{2,3},{3,6},{6,7},{7,... | collective-permute-start | bytes 208904 | tf_op jit(solution)/shard_map/ppermute | solution.py:24
  44.1 24.1 %copy-start.39 = (pred[4,4,24]{2,1,0:T(4,128)(4,1)}, pred[4,4,24]{2,1,0:T(4,128)(4,1)S(1)}, u32[]{:S(2)}) copy-start(pred[4,4,24]{2,1,0:T(4,128)(4,1)S(1)} %gather_fusion.1) | copy-start | bytes 1156
  44.7 24.1 %copy-start.36 = (pred[4,4,24]{2,1,0:T(4,128)(4,1)}, pred[4,4,24]{2,1,0:T(4,128)(4,1)S(1)}, u32[]{:S(2)}) copy-start(pred[4,4,24]{2,1,0:T(4,128)(4,1)S(1)} %gather_fusion) | copy-start | bytes 1156
  62.9 4.3 %collective-permute-start.3 = (bf16[8,64,68]{1,0,2:T(8,128)(2,1)S(1)}, bf16[8,64,68]{1,0,2:T(8,128)(2,1)S(1)}, u32[]{:S(2)}, u32[]{:S(2)}) collective-permute-start(bf16[8,64,68]{1,0,2:T(8,128)(2,1)S(1)} %copy.745), channel_id=1, source_target_pairs={{1,0},{4,1},{5,4},{8,5},{9,8},{12,9},{13,12},{3,2},{6,3},{7,6},{10... | collective-permute-start | bytes 208904 | tf_op jit(solution)/shard_map/ppermute | solution.py:26
  64.2 4.0 %collective-permute-start.2 = (bf16[8,64,68]{1,0,2:T(8,128)(2,1)S(1)}, bf16[8,64,68]{1,0,2:T(8,128)(2,1)S(1)}, u32[]{:S(2)}, u32[]{:S(2)}) collective-permute-start(bf16[8,64,68]{1,0,2:T(8,128)(2,1)S(1)} %copy.745), channel_id=1, source_target_pairs={{0,1},{1,4},{4,5},{5,8},{8,9},{9,12},{12,13},{2,3},{3,6},{6,7},{7,... | collective-permute-start | bytes 208904 | tf_op jit(solution)/shard_map/ppermute | solution.py:24
  87.9 31.0 %copy-start.1 = (bf16[4,64,256]{1,2,0:T(8,128)(2,1)}, bf16[4,64,256]{1,2,0:T(8,128)(2,1)S(1)}, u32[]{:S(2)}) copy-start(bf16[4,64,256]{1,2,0:T(8,128)(2,1)S(1)} %copy.772) | copy-start | bytes 393220
  89.5 18.2 %copy-start.37 = (pred[4,4,24]{2,1,0:T(4,128)(4,1)S(1)}, pred[4,4,24]{2,1,0:T(4,128)(4,1)}, u32[]{:S(2)}) copy-start(pred[4,4,24]{2,1,0:T(4,128)(4,1)} %copy-done.36) | copy-start | bytes 1156
  96.1 8.5 %collective-permute-start.4 = (bf16[8,64,68]{2,0,1:T(8,128)(2,1)}, bf16[8,64,68]{2,0,1:T(8,128)(2,1)}, u32[]{:S(2)}, u32[]{:S(2)}) collective-permute-start(bf16[8,64,68]{2,0,1:T(8,128)(2,1)} %copy.779), channel_id=1, source_target_pairs={{0,1},{1,4},{4,5},{5,8},{8,9},{9,12},{12,13},{2,3},{3,6},{6,7},{7,... | collective-permute-start | bytes 208904 | tf_op jit(solution)/shard_map/ppermute | solution.py:24
  101.7 5.9 %collective-permute-start.5 = (bf16[8,64,68]{2,0,1:T(8,128)(2,1)}, bf16[8,64,68]{2,0,1:T(8,128)(2,1)S(1)}, u32[]{:S(2)}, u32[]{:S(2)}) collective-permute-start(bf16[8,64,68]{2,0,1:T(8,128)(2,1)} %copy.779), channel_id=1, source_target_pairs={{1,0},{4,1},{5,4},{8,5},{9,8},{12,9},{13,12},{3,2},{6,3},{7,6},{10... | collective-permute-start | bytes 208904 | tf_op jit(solution)/shard_map/ppermute | solution.py:26
  104.5 100.4 %reduce-scatter.23.cloned.1.call-start = ((), (), s32[]{:S(2)}) async-start(), calls=%async_computation.13 | async-start | bytes 98304
  133.3 8.1 %copy-start.12 = (bf16[1,4,64,256]{3,2,1,0:T(8,128)(2,1)S(1)}, bf16[1,4,64,256]{3,2,1,0:T(8,128)(2,1)}, u32[]{:S(2)}) copy-start(bf16[1,4,64,256]{3,2,1,0:T(8,128)(2,1)} %copy.801) | copy-start | bytes 393220
  144.9 18.8 %copy-start.2 = (bf16[4,64,256]{2,1,0:T(8,128)(2,1)}, bf16[4,64,256]{2,1,0:T(8,128)(2,1)S(1)}, u32[]{:S(2)}) copy-start(bf16[4,64,256]{2,1,0:T(8,128)(2,1)S(1)} %add_convert_fusion.1) | copy-start | bytes 393220
  145.1 31.9 %copy-start = (bf16[4,64,256]{1,2,0:T(8,128)(2,1)}, bf16[4,64,256]{1,2,0:T(8,128)(2,1)S(1)}, u32[]{:S(2)}) copy-start(bf16[4,64,256]{1,2,0:T(8,128)(2,1)S(1)} %copy.807) | copy-start | bytes 393220
  147.3 18.5 %copy-start.38 = (pred[4,4,24]{2,1,0:T(4,128)(4,1)S(1)}, pred[4,4,24]{2,1,0:T(4,128)(4,1)}, u32[]{:S(2)}) copy-start(pred[4,4,24]{2,1,0:T(4,128)(4,1)} %copy-done.36) | copy-start | bytes 1156
  154.0 9.9 %collective-permute-start.6 = (bf16[8,64,68]{2,0,1:T(8,128)(2,1)}, bf16[8,64,68]{2,0,1:T(8,128)(2,1)}, u32[]{:S(2)}, u32[]{:S(2)}) collective-permute-start(bf16[8,64,68]{2,0,1:T(8,128)(2,1)} %copy.814), channel_id=1, source_target_pairs={{0,1},{1,4},{4,5},{5,8},{8,9},{9,12},{12,13},{2,3},{3,6},{6,7},{7,... | collective-permute-start | bytes 208904 | tf_op jit(solution)/shard_map/ppermute | solution.py:24
  158.9 47.5 %reduce-scatter.21.cloned.1.call-start = ((), (), s32[]{:S(2)}) async-start(), calls=%async_computation.12 | async-start | bytes 98304
  161.0 3.9 %collective-permute-start.7 = (bf16[8,64,68]{2,0,1:T(8,128)(2,1)}, bf16[8,64,68]{2,0,1:T(8,128)(2,1)}, u32[]{:S(2)}, u32[]{:S(2)}) collective-permute-start(bf16[8,64,68]{2,0,1:T(8,128)(2,1)} %copy.814), channel_id=1, source_target_pairs={{1,0},{4,1},{5,4},{8,5},{9,8},{12,9},{13,12},{3,2},{6,3},{7,6},{10... | collective-permute-start | bytes 208904 | tf_op jit(solution)/shard_map/ppermute | solution.py:26
  163.8 49.3 %reduce-scatter.19.cloned.1.call-start = ((), (), s32[]{:S(2)}) async-start(), calls=%async_computation.11 | async-start | bytes 98304
  191.4 8.2 %copy-start.13 = (bf16[1,4,64,256]{3,2,1,0:T(8,128)(2,1)S(1)}, bf16[1,4,64,256]{3,2,1,0:T(8,128)(2,1)}, u32[]{:S(2)}) copy-start(bf16[1,4,64,256]{3,2,1,0:T(8,128)(2,1)} %copy.836) | copy-start | bytes 393220
  201.1 26.3 %reduce-scatter.17.cloned.1.call-start = ((), (), s32[]{:S(2)}) async-start(), calls=%async_computation.10 | async-start | bytes 393216 | tf_op jit(solution)/shard_map/reduce_scatter | solution.py:212
  202.6 38.7 %reduce-scatter.15.cloned.1.call-start = ((), (), s32[]{:S(2)}) async-start(), calls=%async_computation.9 | async-start | bytes 393216 | tf_op jit(solution)/shard_map/reduce_scatter | solution.py:212
  208.9 94.7 %all-to-all-start.2 = ((bf16[4,256,256]{2,0,1:T(4,128)(2,1)}), bf16[4,256,256]{2,0,1:T(4,128)(2,1)S(1)}, u32[]{:S(2)}, u32[]{:S(2)}) async-start(bf16[4,256,256]{2,0,1:T(4,128)(2,1)} %copy.842), calls=%async_computation.2 | async-start | bytes 1048576 | tf_op jit(solution)/shard_map/all_to_all | solution.py:218
  212.4 89.3 %all-reduce.3.cloned.1.call-start = ((), (), s32[]{:S(2)}) async-start(), calls=%async_computation.15 | async-start | bytes 1310720 | tf_op jit(solution)/shard_map/psum | solution.py:245
  (33 other events, 108.4 us)
Sparse Core Ops, SparseCore 0:
  104.6 13.6 reduce-scatter.24
  159.1 9.1 reduce-scatter.22
  171.1 9.8 reduce-scatter.20
  201.2 11.8 reduce-scatter.18
  215.7 11.6 reduce-scatter.16
  229.6 11.6 reduce-scatter.14
  244.4 57.1 all-reduce.2
where the time goes:
time: 315 us; the launch traced here: 313 us
  local copies, waits for them, and re-layouts  105 us (33%)
  waiting for transfers between devices  95.7 us (30%)
  blocking collectives  33.1 us (11%)
  starting transfers between devices  31.3 us (10%)
  other arithmetic  16.7 us (5%)
  between operations  16.3 us (5%)
  matrix products  14.9 us (5%)
    psum x1, waiting for transfers between devices, local(): lax.psum((down_gradient, core_gradient, up_gradient), ('tiles', 'sub'))  58.5 us
    unnamed x148, local copies, waits for them, and re-layouts  27.2 us
    reduce_scatter x2, waiting for transfers between devices, whole_tiles(): lax.psum_scatter(core_part.astype(jnp.bfloat16), 'chan', scatter_dimensio...  26.7 us
    another operation x18, local copies, waits for them, and re-layouts, stacked_windows(): jnp.stack([window(padded, 2 - offset // 3, 2 - offset % 3) for offset in...  25.9 us
    all_gather x4, blocking collectives, padded_of(): owner_cycle = lax.all_gather(border, 'chan', axis=0, tiled=True)  20.2 us
    ppermute x4, starting transfers between devices, padded_2(): lax.ppermute(tail, axis, [(i, (i + 1) % count) for i in range(ends)])  14.7 us
    slice x20, local copies, waits for them, and re-layouts, place_border(): nearest[:, which_side, :, piece_index * TILE:(piece_index + 1) * TILE]  14 us
    another operation x18, local copies, waits for them, and re-layouts, stacked_windows(): jnp.stack([window(padded, offset // 3, offset % 3) for offset in range(9)...  8.55 us
  transfers between devices with their start and end apart: 18, of which 7 were waited for; matrix products, arithmetic and copies ran while one was open for 32% of the time, Pallas kernels for 0%

commit v1 on v0

--- a/solution.py
+++ b/solution.py
@@ -66,13 +66,13 @@
     squares = flat_cells.reshape(flat_cells.shape[0], flat_cells.shape[1], TILE, TILE)
     nearest = jnp.einsum(
         "uvd,dck->uvck",
-        chooser[:, EDGE_ROWS, :],
+        jnp.stack([chooser[:, row] for row in EDGE_ROWS], axis=1),
         extended[:, :, : 4 * TILE],
         preferred_element_type=jnp.float32,
     ).astype(jnp.bfloat16)
     diagonal = jnp.einsum(
         "uvd,dck->uvck",
-        chooser[:, CORNER_ROWS, :],
+        jnp.stack([chooser[:, row] for row in CORNER_ROWS], axis=1),
         extended[:, :, 4 * TILE :],
         preferred_element_type=jnp.float32,
     ).astype(jnp.bfloat16)

time: 315 us -> 321 us (1.019)
    unnamed x148 -> x132, local copies, waits for them, and re-layouts: 27.2 us -> 27.1 us
  transfers between devices with their start and end apart: 18 -> 18, of which waited for: 7 -> 8; matrix products, arithmetic and copies ran while one was open for 32% -> 32% of each run, Pallas kernels for 0% -> 0%
where the time goes in v1:
time: 321 us; the launch traced here: 319 us
  local copies, waits for them, and re-layouts  106 us (33%)
  waiting for transfers between devices  96.8 us (30%)
  starting transfers between devices  34.3 us (11%)
  blocking collectives  33.1 us (10%)
  other arithmetic  16.8 us (5%)
  between operations  16.2 us (5%)
  matrix products  15 us (5%)
    psum x1, waiting for transfers between devices, local(): lax.psum((down_gradient, core_gradient, up_gradient), ('tiles', 'sub'))  58.5 us
    unnamed x132, local copies, waits for them, and re-layouts  27.1 us
    reduce_scatter x2, waiting for transfers between devices, whole_tiles(): lax.psum_scatter(core_part.astype(jnp.bfloat16), 'chan', scatter_dimensio...  26.7 us
    another operation x18, local copies, waits for them, and re-layouts, stacked_windows(): jnp.stack([window(padded, 2 - offset // 3, 2 - offset % 3) for offset in...  25.9 us
    all_gather x4, blocking collectives, padded_of(): owner_cycle = lax.all_gather(border, 'chan', axis=0, tiled=True)  20.2 us
    ppermute x4, starting transfers between devices, padded_2(): lax.ppermute(tail, axis, [(i, (i + 1) % count) for i in range(ends)])  17.6 us
    slice x20, local copies, waits for them, and re-layouts, place_border(): nearest[:, which_side, :, piece_index * TILE:(piece_index + 1) * TILE]  14.6 us
    another operation x18, local copies, waits for them, and re-layouts, stacked_windows(): jnp.stack([window(padded, offset // 3, offset % 3) for offset in range(9)...  8.53 us
  transfers between devices with their start and end apart: 18, of which 8 were waited for; matrix products, arithmetic and copies ran while one was open for 32% of the time, Pallas kernels for 0%

profile of v1, /device:TPU:0, one launch (start us, length us, event | category | flops | bytes accessed | tf_op | source)
XLA Modules:
  0.0 318.6 jit_solution(4942004799345471863)
XLA Ops:
  7.2 4.3 %all-to-all-start.1 = ((bf16[8,128,256]{2,1,0:T(8,128)(2,1)}), bf16[8,128,256]{2,1,0:T(8,128)(2,1)S(1)}, u32[]{:S(2)}, u32[]{:S(2)}) async-start(bf16[8,128,256]{2,1,0:T(8,128)(2,1)} %param.8), calls=%async_computation.1 | async-start | bytes 1048576 | tf_op jit(solution)/shard_map/all_to_all | solution.py:153
  13.7 6.6 %all-to-all-done.1 = bf16[8,128,256]{2,1,0:T(8,128)(2,1)S(1)} async-done(((bf16[8,128,256]{2,1,0:T(8,128)(2,1)}), bf16[8,128,256]{2,1,0:T(8,128)(2,1)S(1)}, u32[]{:S(2)}, u32[]{:S(2)}) %all-to-all-start.1) | async-done | bytes 524320 | tf_op jit(solution)/shard_map/all_to_all | solution.py:153
  20.3 3.5 %all-to-all-start = ((bf16[8,128,256]{2,1,0:T(8,128)(2,1)}), bf16[8,128,256]{2,1,0:T(8,128)(2,1)S(1)}, u32[]{:S(2)}, u32[]{:S(2)}) async-start(bf16[8,128,256]{2,1,0:T(8,128)(2,1)} %param.9), calls=%async_computation | async-start | bytes 1048576 | tf_op jit(solution)/shard_map/all_to_all | solution.py:154
  23.8 8.3 %all_gather.18 = bf16[2,256,64]{1,2,0:T(8,128)(2,1)S(1)} all-gather(bf16[2,128,64]{1,2,0:T(8,128)(2,1)S(1)} %copy-done.36), channel_id=1, replica_groups=mesh['groups'=2,'tiles'=4,'chan'=2,'sub'=2] {'chan'}, dimensions={1}, use_global_device_ids=true | all-gather | bytes 98304 | tf_op jit(solution)/shard_map/all_gather | solution.py:160
  32.2 4.6 %all_gather.20 = bf16[2,256,64]{1,2,0:T(8,128)(2,1)S(1)} all-gather(bf16[2,128,64]{1,2,0:T(8,128)(2,1)S(1)} %copy-done.37), channel_id=1, replica_groups=mesh['groups'=2,'tiles'=4,'chan'=2,'sub'=2] {'chan'}, dimensions={1}, use_global_device_ids=true | all-gather | bytes 98304 | tf_op jit(solution)/shard_map/all_gather | solution.py:161
  38.7 4.9 %all_gather.19 = bf16[8,64,68]{2,1,0:T(8,128)(2,1)S(1)} all-gather(bf16[4,64,68]{2,1,0:T(8,128)(2,1)S(1)} %copy.660), channel_id=1, replica_groups=mesh['groups'=2,'tiles'=4,'chan'=2,'sub'=2] {'chan'}, dimensions={0}, use_global_device_ids=true | all-gather | bytes 104448 | tf_op jit(solution)/shard_map/all_gather | solution.py:169
  45.1 3.0 collective-permute-start
  57.4 4.9 %all_gather.21 = bf16[8,64,68]{2,1,0:T(8,128)(2,1)S(1)} all-gather(bf16[4,64,68]{2,1,0:T(8,128)(2,1)S(1)} %copy.692), channel_id=1, replica_groups=mesh['groups'=2,'tiles'=4,'chan'=2,'sub'=2] {'chan'}, dimensions={0}, use_global_device_ids=true | all-gather | bytes 104448 | tf_op jit(solution)/shard_map/all_gather | solution.py:169
  63.8 3.5 %collective-permute-start.2 = (bf16[8,64,68]{1,0,2:T(8,128)(2,1)S(1)}, bf16[8,64,68]{1,0,2:T(8,128)(2,1)S(1)}, u32[]{:S(2)}, u32[]{:S(2)}) collective-permute-start(bf16[8,64,68]{1,0,2:T(8,128)(2,1)S(1)} %copy.693), channel_id=1, source_target_pairs={{0,1},{1,4},{4,5},{5,8},{8,9},{9,12},{12,13},{2,3},{3,6},{6,7},{7,... | collective-permute-start | bytes 208904 | tf_op jit(solution)/shard_map/ppermute | solution.py:24
  91.6 5.1 %all_gather.22 = bf16[8,64,68]{2,1,0:T(8,128)(2,1)S(1)} all-gather(bf16[4,64,68]{2,1,0:T(8,128)(2,1)} %copy.724), channel_id=1, replica_groups=mesh['groups'=2,'tiles'=4,'chan'=2,'sub'=2] {'chan'}, dimensions={0}, use_global_device_ids=true | all-gather | bytes 104448 | tf_op jit(solution)/shard_map/all_gather | solution.py:169
  97.5 6.0 %collective-permute-start.4 = (bf16[8,64,68]{2,0,1:T(8,128)(2,1)}, bf16[8,64,68]{2,0,1:T(8,128)(2,1)}, u32[]{:S(2)}, u32[]{:S(2)}) collective-permute-start(bf16[8,64,68]{2,0,1:T(8,128)(2,1)} %copy.725), channel_id=1, source_target_pairs={{0,1},{1,4},{4,5},{5,8},{8,9},{9,12},{12,13},{2,3},{3,6},{6,7},{7,... | collective-permute-start | bytes 208904 | tf_op jit(solution)/shard_map/ppermute | solution.py:24
  103.5 1.9 fusion.27
  109.4 2.2 collective-permute-done.5
  112.8 1.9 copy.732
  123.4 1.7 pad_maximum_fusion.10
  137.9 1.8 copy.743
  139.6 1.7 copy.742
  141.4 1.8 copy.741
  154.0 5.1 %all_gather.23 = bf16[8,64,68]{2,1,0:T(8,128)(2,1)S(1)} all-gather(bf16[4,64,68]{2,1,0:T(8,128)(2,1)} %copy.757), channel_id=1, replica_groups=mesh['groups'=2,'tiles'=4,'chan'=2,'sub'=2] {'chan'}, dimensions={0}, use_global_device_ids=true | all-gather | bytes 104448 | tf_op jit(solution)/shard_map/all_gather | solution.py:169
  159.8 4.9 %collective-permute-start.6 = (bf16[8,64,68]{2,0,1:T(8,128)(2,1)}, bf16[8,64,68]{2,0,1:T(8,128)(2,1)}, u32[]{:S(2)}, u32[]{:S(2)}) collective-permute-start(bf16[8,64,68]{2,0,1:T(8,128)(2,1)} %copy.758), channel_id=1, source_target_pairs={{0,1},{1,4},{4,5},{5,8},{8,9},{9,12},{12,13},{2,3},{3,6},{6,7},{7,... | collective-permute-start | bytes 208904 | tf_op jit(solution)/shard_map/ppermute | solution.py:24
  164.9 2.0 fusion.25
  172.8 1.9 copy.765
  191.1 1.7 copy.781
  197.3 1.8 copy.776
  199.1 1.7 copy.775
  200.8 1.8 copy.774
  214.8 3.5 %all-to-all-start.2 = ((bf16[4,256,256]{2,0,1:T(4,128)(2,1)}), bf16[4,256,256]{2,0,1:T(4,128)(2,1)S(1)}, u32[]{:S(2)}, u32[]{:S(2)}) async-start(bf16[4,256,256]{2,0,1:T(4,128)(2,1)} %copy.784), calls=%async_computation.2 | async-start | bytes 1048576 | tf_op jit(solution)/shard_map/all_to_all | solution.py:218
  220.6 12.8 %reduce-scatter.17.cloned.1.call-done = bf16[9,32,64]{2,0,1:T(8,128)(2,1)} async-done(((bf16[9,64,64]{2,0,1:T(8,128)(2,1)}), bf16[9,32,64]{2,0,1:T(8,128)(2,1)}) %reduce-scatter.17.cloned.1.call-update) | async-done | bytes 36880 | tf_op jit(solution)/shard_map/reduce_scatter | solution.py:212
  233.5 13.9 %reduce-scatter.15.cloned.1.call-done = bf16[9,32,64]{2,0,1:T(8,128)(2,1)} async-done(((bf16[9,64,64]{2,0,1:T(8,128)(2,1)}), bf16[9,32,64]{2,0,1:T(8,128)(2,1)}) %reduce-scatter.15.cloned.1.call-update) | async-done | bytes 36880 | tf_op jit(solution)/shard_map/reduce_scatter | solution.py:212
  247.4 1.9 maximum_convert_fusion
  249.2 58.5 %all-reduce.3.cloned.1.call-done = (f32[2,128,64]{1,2,0:T(8,128)}, f32[2,9,32,64]{3,1,2,0:T(8,128)}, f32[2,128,64]{1,2,0:T(8,128)}) async-done(((f32[2,128,64]{1,2,0:T(8,128)}, f32[2,9,32,64]{3,1,2,0:T(8,128)}, f32[2,128,64]{1,2,0:T(8,128)}), (f32[2,128,64]{1,2,0:T(8,128)}, f32[2,9,32,64]{3,1,2,0:T(8,128)}, f32[2,128,64]{1,2,0:T(8,128)})) %all-reduce.3.cloned.1.call-update) | async-done | bytes 278544 | tf_op jit(solution)/shard_map/psum | solution.py:245
  307.7 1.9 copy.788
  (330 shorter events, 121.0 us)
Async XLA Ops:
  7.2 16.7 %copy-start.36 = (bf16[2,128,64]{1,2,0:T(8,128)(2,1)S(1)}, bf16[2,128,64]{1,2,0:T(8,128)(2,1)}, u32[]{:S(2)}) copy-start(bf16[2,128,64]{1,2,0:T(8,128)(2,1)} %param.10) | copy-start | bytes 98308
  7.2 25.0 %copy-start.37 = (bf16[2,128,64]{1,2,0:T(8,128)(2,1)S(1)}, bf16[2,128,64]{1,2,0:T(8,128)(2,1)}, u32[]{:S(2)}) copy-start(bf16[2,128,64]{1,2,0:T(8,128)(2,1)} %param.12) | copy-start | bytes 98308
  7.2 13.1 %all-to-all-start.1 = ((bf16[8,128,256]{2,1,0:T(8,128)(2,1)}), bf16[8,128,256]{2,1,0:T(8,128)(2,1)S(1)}, u32[]{:S(2)}, u32[]{:S(2)}) async-start(bf16[8,128,256]{2,1,0:T(8,128)(2,1)} %param.8), calls=%async_computation.1 | async-start | bytes 1048576 | tf_op jit(solution)/shard_map/all_to_all | solution.py:153
  20.3 16.6 %all-to-all-start = ((bf16[8,128,256]{2,1,0:T(8,128)(2,1)}), bf16[8,128,256]{2,1,0:T(8,128)(2,1)S(1)}, u32[]{:S(2)}, u32[]{:S(2)}) async-start(bf16[8,128,256]{2,1,0:T(8,128)(2,1)} %param.9), calls=%async_computation | async-start | bytes 1048576 | tf_op jit(solution)/shard_map/all_to_all | solution.py:154
  23.8 184.8 %reduce-scatter.25.cloned.1.call-start = ((), (), s32[]{:S(2)}) async-start(), calls=%async_computation.14 | async-start | bytes 98304
  32.2 24.1 %copy-start.26 = (bf16[2,256,64]{1,2,0:T(8,128)(2,1)}, bf16[2,256,64]{1,2,0:T(8,128)(2,1)S(1)}, u32[]{:S(2)}) copy-start(bf16[2,256,64]{1,2,0:T(8,128)(2,1)S(1)} %all_gather.18) | copy-start | bytes 196612
  36.8 17.9 %copy-start.31 = (bf16[2,256,64]{1,2,0:T(8,128)(2,1)}, bf16[2,256,64]{1,2,0:T(8,128)(2,1)S(1)}, u32[]{:S(2)}) copy-start(bf16[2,256,64]{1,2,0:T(8,128)(2,1)S(1)} %all_gather.20) | copy-start | bytes 196612
  43.8 4.4 %collective-permute-start.1 = (bf16[8,64,68]{1,0,2:T(8,128)(2,1)S(1)}, bf16[8,64,68]{1,0,2:T(8,128)(2,1)S(1)}, u32[]{:S(2)}, u32[]{:S(2)}) collective-permute-start(bf16[8,64,68]{1,0,2:T(8,128)(2,1)S(1)} %copy.661), channel_id=1, source_target_pairs={{1,0},{4,1},{5,4},{8,5},{9,8},{12,9},{13,12},{3,2},{6,3},{7,6},{10... | collective-permute-start | bytes 208904 | tf_op jit(solution)/shard_map/ppermute | solution.py:26
  45.1 4.0 %collective-permute-start = (bf16[8,64,68]{1,0,2:T(8,128)(2,1)S(1)}, bf16[8,64,68]{1,0,2:T(8,128)(2,1)S(1)}, u32[]{:S(2)}, u32[]{:S(2)}) collective-permute-start(bf16[8,64,68]{1,0,2:T(8,128)(2,1)S(1)} %copy.661), channel_id=1, source_target_pairs={{0,1},{1,4},{4,5},{5,8},{8,9},{9,12},{12,13},{2,3},{3,6},{6,7},{7,... | collective-permute-start | bytes 208904 | tf_op jit(solution)/shard_map/ppermute | solution.py:24
  62.5 4.8 %collective-permute-start.3 = (bf16[8,64,68]{1,0,2:T(8,128)(2,1)S(1)}, bf16[8,64,68]{1,0,2:T(8,128)(2,1)S(1)}, u32[]{:S(2)}, u32[]{:S(2)}) collective-permute-start(bf16[8,64,68]{1,0,2:T(8,128)(2,1)S(1)} %copy.693), channel_id=1, source_target_pairs={{1,0},{4,1},{5,4},{8,5},{9,8},{12,9},{13,12},{3,2},{6,3},{7,6},{10... | collective-permute-start | bytes 208904 | tf_op jit(solution)/shard_map/ppermute | solution.py:26
  63.8 4.5 %collective-permute-start.2 = (bf16[8,64,68]{1,0,2:T(8,128)(2,1)S(1)}, bf16[8,64,68]{1,0,2:T(8,128)(2,1)S(1)}, u32[]{:S(2)}, u32[]{:S(2)}) collective-permute-start(bf16[8,64,68]{1,0,2:T(8,128)(2,1)S(1)} %copy.693), channel_id=1, source_target_pairs={{0,1},{1,4},{4,5},{5,8},{8,9},{9,12},{12,13},{2,3},{3,6},{6,7},{7,... | collective-permute-start | bytes 208904 | tf_op jit(solution)/shard_map/ppermute | solution.py:24
  80.3 5.7 %copy-start.16 = (bf16[1,4,64,256]{3,2,1,0:T(8,128)(2,1)S(1)}, bf16[1,4,64,256]{3,2,1,0:T(8,128)(2,1)}, u32[]{:S(2)}) copy-start(bf16[1,4,64,256]{3,2,1,0:T(8,128)(2,1)} %copy.716) | copy-start | bytes 393220
  88.0 35.4 %copy-start.1 = (bf16[4,64,256]{1,2,0:T(8,128)(2,1)}, bf16[4,64,256]{1,2,0:T(8,128)(2,1)S(1)}, u32[]{:S(2)}) copy-start(bf16[4,64,256]{1,2,0:T(8,128)(2,1)S(1)} %copy.718) | copy-start | bytes 393220
  97.5 10.8 %collective-permute-start.4 = (bf16[8,64,68]{2,0,1:T(8,128)(2,1)}, bf16[8,64,68]{2,0,1:T(8,128)(2,1)}, u32[]{:S(2)}, u32[]{:S(2)}) collective-permute-start(bf16[8,64,68]{2,0,1:T(8,128)(2,1)} %copy.725), channel_id=1, source_target_pairs={{0,1},{1,4},{4,5},{5,8},{8,9},{9,12},{12,13},{2,3},{3,6},{6,7},{7,... | collective-permute-start | bytes 208904 | tf_op jit(solution)/shard_map/ppermute | solution.py:24
  105.5 6.1 %collective-permute-start.5 = (bf16[8,64,68]{2,0,1:T(8,128)(2,1)}, bf16[8,64,68]{2,0,1:T(8,128)(2,1)S(1)}, u32[]{:S(2)}, u32[]{:S(2)}) collective-permute-start(bf16[8,64,68]{2,0,1:T(8,128)(2,1)} %copy.725), channel_id=1, source_target_pairs={{1,0},{4,1},{5,4},{8,5},{9,8},{12,9},{13,12},{3,2},{6,3},{7,6},{10... | collective-permute-start | bytes 208904 | tf_op jit(solution)/shard_map/ppermute | solution.py:26
  108.3 102.6 %reduce-scatter.23.cloned.1.call-start = ((), (), s32[]{:S(2)}) async-start(), calls=%async_computation.13 | async-start | bytes 98304
  137.8 8.1 %copy-start.14 = (bf16[1,4,64,256]{3,2,1,0:T(8,128)(2,1)S(1)}, bf16[1,4,64,256]{3,2,1,0:T(8,128)(2,1)}, u32[]{:S(2)}) copy-start(bf16[1,4,64,256]{3,2,1,0:T(8,128)(2,1)} %copy.744) | copy-start | bytes 393220
  137.8 8.1 %copy-start.12 = (bf16[1,4,64,256]{3,2,1,0:T(8,128)(2,1)S(1)}, bf16[1,4,64,256]{3,2,1,0:T(8,128)(2,1)}, u32[]{:S(2)}) copy-start(bf16[1,4,64,256]{3,2,1,0:T(8,128)(2,1)} %copy.745) | copy-start | bytes 393220
  141.4 4.8 %copy-start.17 = (bf16[1,4,64,256]{3,2,1,0:T(8,128)(2,1)S(1)}, bf16[1,4,64,256]{3,2,1,0:T(8,128)(2,1)}, u32[]{:S(2)}) copy-start(bf16[1,4,64,256]{3,2,1,0:T(8,128)(2,1)} %copy.748) | copy-start | bytes 393220
  149.5 20.1 %copy-start.2 = (bf16[4,64,256]{2,1,0:T(8,128)(2,1)}, bf16[4,64,256]{2,1,0:T(8,128)(2,1)S(1)}, u32[]{:S(2)}) copy-start(bf16[4,64,256]{2,1,0:T(8,128)(2,1)S(1)} %add_convert_fusion.1) | copy-start | bytes 393220
  149.7 33.2 %copy-start = (bf16[4,64,256]{1,2,0:T(8,128)(2,1)}, bf16[4,64,256]{1,2,0:T(8,128)(2,1)S(1)}, u32[]{:S(2)}) copy-start(bf16[4,64,256]{1,2,0:T(8,128)(2,1)S(1)} %copy.751) | copy-start | bytes 393220
  159.8 9.8 %collective-permute-start.6 = (bf16[8,64,68]{2,0,1:T(8,128)(2,1)}, bf16[8,64,68]{2,0,1:T(8,128)(2,1)}, u32[]{:S(2)}, u32[]{:S(2)}) collective-permute-start(bf16[8,64,68]{2,0,1:T(8,128)(2,1)} %copy.758), channel_id=1, source_target_pairs={{0,1},{1,4},{4,5},{5,8},{8,9},{9,12},{12,13},{2,3},{3,6},{6,7},{7,... | collective-permute-start | bytes 208904 | tf_op jit(solution)/shard_map/ppermute | solution.py:24
  164.8 47.6 %reduce-scatter.21.cloned.1.call-start = ((), (), s32[]{:S(2)}) async-start(), calls=%async_computation.12 | async-start | bytes 98304
  166.8 3.9 %collective-permute-start.7 = (bf16[8,64,68]{2,0,1:T(8,128)(2,1)}, bf16[8,64,68]{2,0,1:T(8,128)(2,1)}, u32[]{:S(2)}, u32[]{:S(2)}) collective-permute-start(bf16[8,64,68]{2,0,1:T(8,128)(2,1)} %copy.758), channel_id=1, source_target_pairs={{1,0},{4,1},{5,4},{8,5},{9,8},{12,9},{13,12},{3,2},{6,3},{7,6},{10... | collective-permute-start | bytes 208904 | tf_op jit(solution)/shard_map/ppermute | solution.py:26
  169.6 49.5 %reduce-scatter.19.cloned.1.call-start = ((), (), s32[]{:S(2)}) async-start(), calls=%async_computation.11 | async-start | bytes 98304
  197.3 8.1 %copy-start.15 = (bf16[1,4,64,256]{3,2,1,0:T(8,128)(2,1)S(1)}, bf16[1,4,64,256]{3,2,1,0:T(8,128)(2,1)}, u32[]{:S(2)}) copy-start(bf16[1,4,64,256]{3,2,1,0:T(8,128)(2,1)} %copy.777) | copy-start | bytes 393220
  197.3 8.1 %copy-start.3 = (bf16[4,64,256]{2,1,0:T(8,128)(2,1)S(1)}, bf16[4,64,256]{2,1,0:T(8,128)(2,1)}, u32[]{:S(2)}) copy-start(bf16[4,64,256]{2,1,0:T(8,128)(2,1)} %copy-done.2) | copy-start | bytes 393220
  197.3 8.2 %copy-start.13 = (bf16[1,4,64,256]{3,2,1,0:T(8,128)(2,1)S(1)}, bf16[1,4,64,256]{3,2,1,0:T(8,128)(2,1)}, u32[]{:S(2)}) copy-start(bf16[1,4,64,256]{3,2,1,0:T(8,128)(2,1)} %copy.778) | copy-start | bytes 393220
  207.0 26.5 %reduce-scatter.17.cloned.1.call-start = ((), (), s32[]{:S(2)}) async-start(), calls=%async_computation.10 | async-start | bytes 393216 | tf_op jit(solution)/shard_map/reduce_scatter | solution.py:212
  208.5 38.9 %reduce-scatter.15.cloned.1.call-start = ((), (), s32[]{:S(2)}) async-start(), calls=%async_computation.9 | async-start | bytes 393216 | tf_op jit(solution)/shard_map/reduce_scatter | solution.py:212
  214.8 94.8 %all-to-all-start.2 = ((bf16[4,256,256]{2,0,1:T(4,128)(2,1)}), bf16[4,256,256]{2,0,1:T(4,128)(2,1)S(1)}, u32[]{:S(2)}, u32[]{:S(2)}) async-start(bf16[4,256,256]{2,0,1:T(4,128)(2,1)} %copy.784), calls=%async_computation.2 | async-start | bytes 1048576 | tf_op jit(solution)/shard_map/all_to_all | solution.py:218
  218.3 89.4 %all-reduce.3.cloned.1.call-start = ((), (), s32[]{:S(2)}) async-start(), calls=%async_computation.15 | async-start | bytes 1310720 | tf_op jit(solution)/shard_map/psum | solution.py:245
  (25 other events, 58.8 us)
Sparse Core Ops, SparseCore 0:
  108.4 13.9 reduce-scatter.24
  164.9 9.3 reduce-scatter.22
  177.1 9.8 reduce-scatter.20
  207.1 11.9 reduce-scatter.18
  221.8 11.6 reduce-scatter.16
  235.6 11.6 reduce-scatter.14
  250.5 57.1 all-reduce.2

commit v2 on v1

v2 whole, which is shorter than its diff:
```python
import functools

import jax
import jax.numpy as jnp
import numpy as np
from jax import lax
from jax.experimental import pallas as pl
from jax.experimental.pallas import tpu as pltpu
from jax.sharding import PartitionSpec as P

TILE = 16
PIX = TILE * TILE
LAYERS = 2
HALO = 128
LANE_DIRECTIONS = [(6, 16), (1, 16), (4, 16), (3, 16), (7, 1), (5, 1), (2, 1), (0, 1)]
F32, BF16 = jnp.float32, jnp.bfloat16
MESH = pl.DeviceIdType.MESH


def border_matrix():
    chosen = np.zeros((PIX, HALO), np.float32)
    last = TILE - 1
    for k in range(TILE):
        chosen[k, k] = 1
        chosen[last * TILE + k, TILE + k] = 1
        chosen[k * TILE, 2 * TILE + k] = 1
        chosen[k * TILE + last, 3 * TILE + k] = 1
    for lane, pixel in enumerate((0, last, last * TILE, PIX - 1)):
        chosen[pixel, 4 * TILE + lane] = 1
    return chosen


def window_matrix():
    chosen = np.zeros((PIX + HALO, 9, TILE, TILE), np.float32)
    end = TILE + 1
    for tap in range(9):
        for i in range(TILE):
            for j in range(TILE):
                row, col = i + tap // 3, j + tap % 3
                if 0 < row < end and 0 < col < end:
                    source = (row - 1) * TILE + col - 1
                elif 0 < col < end:
                    source = PIX + (TILE if row == 0 else 0) + col - 1
                elif 0 < row < end:
                    source = PIX + (3 * TILE if col == 0 else 2 * TILE) + row - 1
                else:
                    source = PIX + 4 * TILE + (2 if row == 0 else 0) + (1 if col == 0 else 0)
                chosen[source, tap, i, j] = 1
    return chosen.reshape(PIX + HALO, 9 * PIX)


def nn(a, b):
    return jnp.dot(a, b, preferred_element_type=F32)


def nt(a, b):
    return lax.dot_general(a, b, (((1,), (1,)), ((), ())), preferred_element_type=F32)


def tn(a, b):
    return lax.dot_general(a, b, (((0,), (0,)), ((), ())), preferred_element_type=F32)


def kernel(
    sizes, feat, cot, down, up, kf, kb, alive, chooser, bsel, wsel,
    out, dgrad, ugrad, cgrad,
    inbox, fact, hid, grad_e, zs, bs, wins, mwin, border, ext, stage, outbox, gsend, grecv, csend, crecv, cown,
    send_sem, recv_sem, bsend_sem, brecv_sem,
):
    tiles, subs, members, here = sizes
    chan = lax.axis_index("chan")
    owner = lax.axis_index("tiles") * subs + lax.axis_index("sub")
    owners = tiles * subs
    has_prev, has_next = owner > 0, owner < owners - 1
    rank = down.shape[2]
    part = rank // members

    def peer(j):
        return (chan + j) % members

    def at(shift, c):
        o = owner + shift
        return {"tiles": o // subs, "sub": o % subs, "chan": c}

    near = [
        (shift, j, cond)
        for shift, cond in ((0, None), (1, has_next), (-1, has_prev))
        for j in range(members)
        if shift or j
    ]

    def guarded(cond, action):
        if cond is None:
            action()
        else:
            pl.when(cond)(action)

    @pl.when(jnp.logical_not(has_prev))
    def _():
        ext[:, 0] = jnp.zeros_like(ext[:, 0])

    @pl.when(jnp.logical_not(has_next))
    def _():
        ext[:, 2] = jnp.zeros_like(ext[:, 2])

    barrier = pltpu.get_barrier_semaphore()
    for shift, j, cond in near:
        def greet(shift=shift, j=j):
            pl.semaphore_signal(barrier, inc=1, device_id=at(shift, peer(j)), device_id_type=MESH)
        guarded(cond, greet)
    sides = has_prev.astype(jnp.int32) + has_next.astype(jnp.int32)
    pl.semaphore_wait(barrier, members - 1 + members * sides)

    def to_peer(k, j, src, dst):
        return pltpu.make_async_remote_copy(
            src_ref=src, dst_ref=dst, send_sem=send_sem.at[k, j], recv_sem=recv_sem.at[k, members - j],
            device_id={"chan": peer(j)}, device_id_type=MESH,
        )

    def from_peer(k, j, src, dst):
        return pltpu.make_async_remote_copy(
            src_ref=src, dst_ref=dst, send_sem=send_sem.at[k, j], recv_sem=recv_sem.at[k, j],
            device_id={"chan": peer(j)}, device_id_type=MESH,
        )

    def slots_of(j):
        return pl.ds(peer(j) * here, here)

    peers = range(1, members)
    sent, arrivals = [], {}

    def exchange(k, source, target):
        for j in peers:
            sent.append(to_peer(k, j, source(j), target.at[members - j]))
            sent[-1].start()
        arrivals[k] = [from_peer(k, j, source(j), target.at[j]) for j in peers]

    def arrived(k):
        for copy in arrivals[k]:
            copy.wait_recv()

    exchange(0, lambda j: down, fact.at[0])
    exchange(1, lambda j: feat.at[slots_of(j)], inbox.at[0])
    exchange(2, lambda j: up, fact.at[1])
    exchange(3, lambda j: cot.at[slots_of(j)], inbox.at[1])

    def lanes(x):
        return jnp.concatenate([x[u] for u in range(here)], axis=1)

    def live(x):
        return (lanes(x).astype(F32) * alive[...]).astype(BF16)

    hid[0, 0] = live(feat[slots_of(0)])
    grad_e[0] = live(cot[slots_of(0)])

    def field(factors, blocks):
        total = None
        for factor, block in zip(factors, blocks):
            part = tn(factor, block).astype(BF16).astype(F32)
            total = part if total is None else total + part
        return total.astype(BF16)

    def place(shift, j):
        return shift % 3 * members + j

    def border_copy(r, k):
        shift, j, cond = near[k]
        mirrored = place(-shift, (members - j) % members)
        return cond, pltpu.make_async_remote_copy(
            src_ref=border.at[r], dst_ref=ext.at[r, 1 - shift, chan],
            send_sem=bsend_sem.at[r, place(shift, j)], recv_sem=brecv_sem.at[r, mirrored],
            device_id=at(shift, peer(j)), device_id_type=MESH,
        )

    def border_arrival(r, k):
        shift, j, cond = near[k]
        return cond, pltpu.make_async_remote_copy(
            src_ref=border.at[r], dst_ref=ext.at[r, 1 + shift, peer(j)],
            send_sem=bsend_sem.at[r, place(shift, j)], recv_sem=brecv_sem.at[r, place(shift, j)],
            device_id=at(shift, peer(j)), device_id_type=MESH,
        )

    def send_border(r, rows):
        edge = nn(rows, bsel[...]).astype(BF16).reshape(here, rank, HALO)
        border[r] = edge
        for k in range(len(near)):
            cond, copy = border_copy(r, k)
            guarded(cond, copy.start)
        ext[r, 1, pl.ds(chan, 1)] = edge[None]

    def finish_border(r):
        for k in range(len(near)):
            cond, copy = border_arrival(r, k)
            guarded(cond, copy.wait_recv)

    def drain_border(r):
        for k in range(len(near)):
            cond, copy = border_copy(r, k)
            guarded(cond, copy.wait_send)

    def rows_of(value):
        return jnp.concatenate([value[:, u * PIX:(u + 1) * PIX] for u in range(here)], axis=0)

    def windows(r, rows, target):
        halos = [jnp.zeros((rank, HALO), F32) for _ in range(here)]
        for v in range(3 * members * here):
            piece = ext[r, v // (members * here), v // here % members, v % here].astype(F32)
            for u in range(here):
                w = u * 3 * members * here + v
                halos[u] = halos[u] + piece * chooser[w:w + 1, :]
        halo = jnp.concatenate(halos, axis=0).astype(BF16)
        both = jnp.concatenate([rows, halo], axis=1)
        for tap in range(9):
            moved = nn(both, wsel[:, tap * PIX:(tap + 1) * PIX]).astype(BF16)
            for u in range(here):
                target[tap * rank:(tap + 1) * rank, u * PIX:(u + 1) * PIX] = moved[u * rank:(u + 1) * rank]

    def factors(which, layer):
        own = (down, up)[which]
        return [own[layer]] + [fact[which, j, layer] for j in peers]

    arrived(0)
    arrived(1)
    for j in peers:
        hid[0, j] = live(inbox[0, j])
    for layer in range(LAYERS):
        act = field(factors(0, layer), [hid[layer, j] for j in range(members)])
        rows = rows_of(act)
        send_border(layer, rows)
        finish_border(layer)
        windows(layer, rows, wins.at[layer])
        b = nn(kf[layer], wins[layer]).astype(BF16)
        bs[layer] = b
        if layer == 0:
            arrived(2)
            arrived(3)
            for j in peers:
                grad_e[j] = live(inbox[1, j])
        for j, factor in enumerate(factors(1, layer)):
            z = nn(factor, b)
            zs[layer, j] = z
            if layer < LAYERS - 1:
                silu = z * jax.nn.sigmoid(z)
                hid[layer + 1, j] = (hid[layer, j].astype(F32) + silu).astype(BF16)
    for layer in reversed(range(LAYERS)):
        r = LAYERS + layer
        deltas = []
        for j in range(members):
            z = zs[layer, j]
            sig = jax.nn.sigmoid(z)
            e = grad_e[j].astype(F32)
            deltas.append((e * sig * (1.0 + z * (1.0 - sig))).astype(BF16))
        m = field(factors(1, layer), deltas)
        rows = rows_of(m)
        send_border(r, rows)
        core = nt(m, wins[layer])
        for c in range(members):
            piece = core[c * part:(c + 1) * part]
            cown[layer, c] = piece
            csend[layer, c] = piece.astype(BF16)
        exchange(5 + 3 * layer, lambda j: csend.at[layer, peer(j)], crecv.at[layer])
        ugrad[layer] = nt(deltas[0], bs[layer])
        for j in peers:
            gsend[layer, 1, j] = nt(deltas[j], bs[layer]).astype(BF16)
        exchange(6 + 3 * layer, lambda j: gsend.at[layer, 1, j], grecv.at[layer, 1])
        finish_border(r)
        windows(r, rows, mwin)
        n = nn(kb[layer], mwin[...]).astype(BF16)
        through_factors = factors(0, layer)
        for j in (*peers, 0):
            new_e = (grad_e[j].astype(F32) + nn(through_factors[j], n)).astype(BF16)
            if layer > 0:
                grad_e[j] = new_e
                continue
            for u in range(here):
                tile = new_e[:, u * PIX:(u + 1) * PIX]
                if j:
                    stage[j, u] = tile
                else:
                    out[pl.ds(chan * here + u, 1)] = tile[None]
            if j == members - 1:
                exchange(4, lambda i: stage.at[i], outbox)
        for j in peers:
            gsend[layer, 0, j] = nt(hid[layer, j], n).astype(BF16)
        exchange(7 + 3 * layer, lambda j: gsend.at[layer, 0, j], grecv.at[layer, 0])
        dgrad[layer] = nt(hid[layer, 0], n)
    for layer in reversed(range(LAYERS)):
        for k in range(3):
            arrived(5 + 3 * layer + k)
        total = cown[layer, pl.ds(chan, 1)][0]
        for j in peers:
            dgrad[layer] = dgrad[layer] + grecv[layer, 0, j].astype(F32)
            ugrad[layer] = ugrad[layer] + grecv[layer, 1, j].astype(F32)
            total = total + crecv[layer, j].astype(F32)
        cgrad[layer] = total
    arrived(4)
    for j in peers:
        for u in range(here):
            out[pl.ds(peer(j) * here + u, 1)] = outbox[j, u][None]
    for copy in sent:
        copy.wait_send()
    for r in range(2 * LAYERS):
        drain_border(r)


def local(sizes, features, cotangent, down_factor, core_kernel, up_factor, tile_count, neighbour_owner, neighbour_slot):
    tiles, subs, members = sizes
    slots, width, _ = features.shape
    here = slots // members
    rank = down_factor.shape[2]
    device = lax.axis_index(("tiles", "sub"))
    first = lax.axis_index("chan") * here
    owner = lax.dynamic_slice_in_dim(neighbour_owner, first, here, 0)
    slot = lax.dynamic_slice_in_dim(neighbour_slot, first, here, 0)
    row = jnp.where(owner >= 0, (owner - device + 1) * slots + slot, -1)
    lane_row = jnp.concatenate(
        [jnp.broadcast_to(row[:, d:d + 1], (here, n)) for d, n in LANE_DIRECTIONS]
        + [jnp.full((here, HALO - 4 * TILE - 4), -1, jnp.int32)],
        axis=1,
    )
    chooser = (lane_row[:, None, :] == jnp.arange(3 * slots)[None, :, None]).astype(F32).reshape(here * 3 * slots, HALO)
    alive = (first + jnp.arange(here * PIX) // PIX < tile_count[0]).astype(F32)[None]
    kf = core_kernel.transpose(0, 2, 1, 3).reshape(LAYERS, rank, 9 * rank)
    kb = core_kernel[:, ::-1].transpose(0, 3, 1, 2).reshape(LAYERS, rank, 9 * rank)
    pixels = here * PIX
    vmem = pl.BlockSpec(memory_space=pltpu.VMEM)
    dma = pltpu.SemaphoreType.DMA
    out, dgrad, ugrad, cgrad = pl.pallas_call(
        functools.partial(kernel, (tiles, subs, members, here)),
        out_shape=(
            jax.ShapeDtypeStruct(features.shape, BF16),
            jax.ShapeDtypeStruct((LAYERS, width, rank), F32),
            jax.ShapeDtypeStruct((LAYERS, width, rank), F32),
            jax.ShapeDtypeStruct((LAYERS, rank // members, 9 * rank), F32),
        ),
        in_specs=[vmem] * 10,
        out_specs=(vmem,) * 4,
        scratch_shapes=[
            pltpu.VMEM((2, members, here, width, PIX), BF16),
            pltpu.VMEM((2, members, LAYERS, width, rank), BF16),
            pltpu.VMEM((LAYERS, members, width, pixels), BF16),
            pltpu.VMEM((members, width, pixels), BF16),
            pltpu.VMEM((LAYERS, members, width, pixels), F32),
            pltpu.VMEM((LAYERS, rank, pixels), BF16),
            pltpu.VMEM((LAYERS, 9 * rank, pixels), BF16),
            pltpu.VMEM((9 * rank, pixels), BF16),
            pltpu.VMEM((2 * LAYERS, here, rank, HALO), BF16),
            pltpu.VMEM((2 * LAYERS, 3, members, here, rank, HALO), BF16),
            pltpu.VMEM((members, here, width, PIX), BF16),
            pltpu.VMEM((members, here, width, PIX), BF16),
            pltpu.VMEM((LAYERS, 2, members, width, rank), BF16),
            pltpu.VMEM((LAYERS, 2, members, width, rank), BF16),
            pltpu.VMEM((LAYERS, members, rank // members, 9 * rank), BF16),
            pltpu.VMEM((LAYERS, members, rank // members, 9 * rank), BF16),
            pltpu.VMEM((LAYERS, members, rank // members, 9 * rank), F32),
            dma((5 + 3 * LAYERS, members)),
            dma((5 + 3 * LAYERS, members)),
            dma((2 * LAYERS, 3 * members)),
            dma((2 * LAYERS, 3 * members)),
        ],
        compiler_params=pltpu.CompilerParams(
            collective_id=0, has_side_effects=True, vmem_limit_bytes=48 * 2**20
        ),
    )(
        features, cotangent, down_factor, up_factor, kf, kb, alive, chooser,
        jnp.asarray(border_matrix(), BF16), jnp.asarray(window_matrix(), BF16),
    )
    dgrad, ugrad, cgrad = lax.psum((dgrad, ugrad, cgrad), ("tiles", "sub"))
    cgrad = cgrad.reshape(LAYERS, rank // members, 9, rank).transpose(0, 2, 1, 3)
    return out, dgrad, cgrad, ugrad


def solution(mesh):
    return jax.shard_map(
        functools.partial(local, tuple(mesh.shape[a] for a in ("tiles", "sub", "chan"))),
        mesh=mesh,
        in_specs=(
            P(("groups", "tiles", "sub"), "chan", None),
            P(("groups", "tiles", "sub"), "chan", None),
            P(None, "chan", None),
            P(),
            P(None, "chan", None),
            P(("groups", "tiles", "sub")),
            P(("groups", "tiles", "sub"), None),
            P(("groups", "tiles", "sub"), None),
        ),
        out_specs=(
            P(("groups", "tiles", "sub"), "chan", None),
            P("groups", "chan", None),
            P("groups", None, "chan", None),
            P("groups", "chan", None),
        ),
        check_vma=False,
    )
```

time: 321 us -> 146 us (0.45)
  local copies, waits for them, and re-layouts: 106 us -> 14.1 us
  Pallas kernels: 0 us -> 54.2 us
  waiting for transfers between devices: 96.8 us -> 61.6 us
  starting transfers between devices: 34.3 us -> 0.04 us
  blocking collectives: 33.1 us -> 0 us
  other arithmetic: 16.8 us -> 0.81 us
  matrix products: 15 us -> 0 us
    pallas_call x0 -> x1, Pallas kernels: none -> 54.2 us  [local(): pl.pallas_call(functools.partial(kernel, (tiles, subs, members, here)), o...]
    another operation x52 -> x0, local copies, waits for them, and re-layouts: 38.4 us -> none  [the longest x18 25.9 us: stacked_windows(): jnp.stack([window(padded, 2 - offset // 3, 2 - offset % 3) for offset in...]
    all_gather x6 -> x0, blocking collectives: 33.1 us -> none  [the longest x4 20.2 us: padded_of(): owner_cycle = lax.all_gather(border, 'chan', axis=0, tiled=True)]
    slice x40 -> x1, local copies, waits for them, and re-layouts: 27.3 us -> 0.22 us  [local(): row[:, d:d + 1]]
    reduce_scatter x2 -> x0, waiting for transfers between devices: 26.7 us -> none  [whole_tiles(): lax.psum_scatter(core_part.astype(jnp.bfloat16), 'chan', scatter_dimensio...]
    ppermute x8 -> x0, starting transfers between devices: 22.7 us -> none  [the longest x4 17.6 us: padded_2(): lax.ppermute(tail, axis, [(i, (i + 1) % count) for i in range(ends)])]
    unnamed x132 -> x18, local copies, waits for them, and re-layouts: 27.1 us -> 9.98 us
    dot_general x30 -> x0, matrix products: 15 us -> none  [the longest x2 2.25 us: whole_tiles(): jnp.einsum('ucq,urq->cr', hidden, act_gradient, preferred_element_type=jn...]
  transfers between devices with their start and end apart: 18 -> 1, of which waited for: 8 -> 1; matrix products, arithmetic and copies ran while one was open for 32% -> 0% of each run, Pallas kernels for 0% -> 0%
where the time goes in v2:
time: 146 us
  waiting for transfers between devices  61.6 us (42%)
  Pallas kernels  54.2 us (37%)
  between operations  15 us (10%)
  local copies, waits for them, and re-layouts  14.1 us (10%)
    psum x1, waiting for transfers between devices, local(): dgrad, ugrad, cgrad = lax.psum((dgrad, ugrad, cgrad), ('tiles', 'sub'))  61.6 us
    pallas_call x1, Pallas kernels, local(): pl.pallas_call(functools.partial(kernel, (tiles, subs, members, here)), o...  54.2 us
    unnamed x18, local copies, waits for them, and re-layouts  9.98 us
  transfers between devices with their start and end apart: 1, of which 1 were waited for; matrix products, arithmetic and copies ran while one was open for 0% of the time, Pallas kernels for 0%

profile of v2, /device:TPU:0, one launch (start us, length us, event | category | flops | bytes accessed | tf_op | source)
XLA Modules:
  0.0 145.6 jit_solution(14550302871250105193)
XLA Ops:
  7.2 0.0 copy-start
  7.2 0.0 copy-start.5
  7.2 0.0 copy-start.1
  7.2 0.0 all-reduce.3.cloned.1.call-start
  8.1 0.1 eq.23
  8.2 0.7 add_select_fusion
  8.9 0.2 fusion.2
  9.1 0.9 copy.22.down
  10.0 0.9 copy.23.up
  10.9 1.0 rev.3
  11.9 1.2 copy.21
  13.0 0.2 copy.24.kf
  13.2 0.2 copy.25.kb
  13.4 0.1 broadcast_in_dim.40
  13.5 0.1 broadcast_in_dim.42
  13.5 0.1 broadcast_in_dim.44
  13.6 0.1 broadcast_in_dim.46
  13.7 0.1 concatenate.3
  13.8 0.1 fusion.chooser
  13.9 0.0 copy-start.2
  13.9 1.0 copy-done.2
  14.9 54.2 %shard_map.129 = (bf16[8,128,256]{2,1,0:T(8,128)(2,1)S(1)}, f32[2,128,64]{2,1,0:T(8,128)S(1)}, f32[2,128,64]{2,1,0:T(8,128)S(1)}, f32[2,32,576]{2,1,0:T(8,128)S(1)}) custom-call(bf16[8,128,256]{2,1,0:T(8,128)(2,1)S(1)} %copy-done.1, bf16[8,128,256]{2,1,0:T(8,128)(2,1)S(1)} %copy-done.2, bf16[2,128,64]{2,1,0:T(8,128)(2,1)S(1)} %copy.22.down, ...), custom_call_target="tpu_custom_call" | custom-call | tf_op jit(solution)/shard_map/pallas_call | solution.py:328
  69.1 0.0 copy-start.3
  69.2 0.6 copy-done.3
  69.8 0.6 copy-done.4
  70.4 0.9 reshape.66
  71.3 0.0 all-reduce.3.cloned.1.call-update
  71.4 61.6 %all-reduce.3.cloned.1.call-done = (f32[2,128,64]{2,1,0:T(8,128)}, f32[2,9,32,64]{3,1,2,0:T(8,128)}, f32[2,128,64]{2,1,0:T(8,128)}) async-done(((f32[2,128,64]{2,1,0:T(8,128)}, f32[2,9,32,64]{3,1,2,0:T(8,128)}, f32[2,128,64]{2,1,0:T(8,128)}), (f32[2,128,64]{2,1,0:T(8,128)}, f32[2,9,32,64]{3,1,2,0:T(8,128)}, f32[2,128,64]{2,1,0:T(8,128)})) %all-reduce.3.cloned.1.call-update) | async-done | bytes 278544 | tf_op jit(solution)/shard_map/psum | solution.py:368
  132.9 1.6 %copy.26 = f32[2,128,64]{1,2,0:T(8,128)} copy(f32[2,128,64]{2,1,0:T(8,128)} %get-tuple-element.24) | data formatting | bytes 131072
  134.5 1.6 %copy.28 = f32[2,128,64]{1,2,0:T(8,128)} copy(f32[2,128,64]{2,1,0:T(8,128)} %get-tuple-element.26) | data formatting | bytes 131072
  136.2 1.8 %copy.27 = f32[2,9,32,64]{3,2,1,0:T(8,128)} copy(f32[2,9,32,64]{3,1,2,0:T(8,128)} %get-tuple-element.25) | data formatting | bytes 294912
  138.0 0.8 copy.34
  (7 shorter events, 0.0 us)
Async XLA Ops:
  7.2 6.7 %copy-start = (bf16[384,2304]{1,0:T(8,128)(2,1)S(1)}, bf16[384,2304]{1,0:T(8,128)(2,1)}, u32[]{:S(2)}) copy-start(bf16[384,2304]{1,0:T(8,128)(2,1)} %constant.45.clone.wsel) | copy-start | bytes 5308420
  7.2 6.7 %copy-start.5 = (bf16[256,128]{1,0:T(8,128)(2,1)S(1)}, bf16[256,128]{1,0:T(8,128)(2,1)}, u32[]{:S(2)}) copy-start(bf16[256,128]{1,0:T(8,128)(2,1)} %constant.44.clone.bsel) | copy-start | bytes 196612
  7.2 6.7 %copy-start.1 = (bf16[8,128,256]{2,1,0:T(8,128)(2,1)S(1)}, bf16[8,128,256]{2,1,0:T(8,128)(2,1)}, u32[]{:S(2)}) copy-start(bf16[8,128,256]{2,1,0:T(8,128)(2,1)} %feat.1) | copy-start | bytes 1572868
  7.2 125.7 %all-reduce.3.cloned.1.call-start = ((), (), s32[]{:S(2)}) async-start(), calls=%async_computation | async-start | bytes 1572864 | tf_op jit(solution)/shard_map/psum | solution.py:368
  13.9 1.0 copy-start.2
  69.1 0.7 copy-start.3
  69.8 0.6 copy-start.4
Sparse Core Ops, SparseCore 0:
  71.5 61.3 all-reduce.2

commit v3 on v2

--- a/solution.py
+++ b/solution.py
@@ -65,7 +65,8 @@
     sizes, feat, cot, down, up, kf, kb, alive, chooser, bsel, wsel,
     out, dgrad, ugrad, cgrad,
     inbox, fact, hid, grad_e, zs, bs, wins, mwin, border, ext, stage, outbox, gsend, grecv, csend, crecv, cown,
-    send_sem, recv_sem, bsend_sem, brecv_sem,
+    dpart, upart, packed, pieces, reduced, whole,
+    send_sem, recv_sem, bsend_sem, brecv_sem, rsend_sem, rrecv_sem,
 ):
     tiles, subs, members, here = sizes
     chan = lax.axis_index("chan")
@@ -89,6 +90,9 @@
         if shift or j
     ]
 
+    def at_owner(o):
+        return {"tiles": o // subs, "sub": o % subs}
+
     def guarded(cond, action):
         if cond is None:
             action()
@@ -104,12 +108,16 @@
         ext[:, 2] = jnp.zeros_like(ext[:, 2])
 
     barrier = pltpu.get_barrier_semaphore()
+    for step in range(1, owners):
+        pl.semaphore_signal(barrier, inc=1, device_id=at_owner((owner + step) % owners), device_id_type=MESH)
     for shift, j, cond in near:
+        if not j:
+            continue
         def greet(shift=shift, j=j):
             pl.semaphore_signal(barrier, inc=1, device_id=at(shift, peer(j)), device_id_type=MESH)
         guarded(cond, greet)
     sides = has_prev.astype(jnp.int32) + has_next.astype(jnp.int32)
-    pl.semaphore_wait(barrier, members - 1 + members * sides)
+    pl.semaphore_wait(barrier, owners - 1 + (members - 1) * (1 + sides))
 
     def to_peer(k, j, src, dst):
         return pltpu.make_async_remote_copy(
@@ -214,6 +222,54 @@
             moved = nn(both, wsel[:, tap * PIX:(tap + 1) * PIX]).astype(BF16)
             for u in range(here):
                 target[tap * rank:(tap + 1) * rank, u * PIX:(u + 1) * PIX] = moved[u * rank:(u + 1) * rank]
+
+    def scatter(layer):
+        for k in range(3):
+            arrived(5 + 3 * layer + k)
+        down_sum, up_sum = dpart[layer], upart[layer]
+        core_sum = cown[layer, pl.ds(chan, 1)][0]
+        for j in peers:
+            down_sum = down_sum + grecv[layer, 0, j].astype(F32)
+            up_sum = up_sum + grecv[layer, 1, j].astype(F32)
+            core_sum = core_sum + crecv[layer, j].astype(F32)
+        spare = whole.shape[1] * whole.shape[2] - down_sum.shape[0] - 5 * part
+        core_sum = jnp.concatenate([core_sum, jnp.zeros((part, rank), F32)], axis=1)
+        lines = [jnp.concatenate([down_sum, up_sum], axis=1)]
+        lines += [core_sum[:, k * 2 * rank:(k + 1) * 2 * rank] for k in range(5)]
+        if spare:
+            lines.append(jnp.zeros((spare, 2 * rank), F32))
+        packed[layer] = jnp.concatenate(lines, axis=0).astype(BF16).reshape(packed.shape[1:])
+        for i in range(1, owners):
+            owner_copy(0, layer, i, packed.at[layer, (owner + i) % owners], pieces.at[layer, owners - i]).start()
+
+    def owner_copy(stage_at, layer, i, src, dst, arriving=False):
+        return pltpu.make_async_remote_copy(
+            src_ref=src, dst_ref=dst, send_sem=rsend_sem.at[stage_at, layer, i],
+            recv_sem=rrecv_sem.at[stage_at, layer, i if arriving else owners - i],
+            device_id=at_owner((owner + i) % owners), device_id_type=MESH,
+        )
+
+    def gather(layer):
+        total = packed[layer, pl.ds(owner, 1)][0].astype(F32)
+        for i in range(1, owners):
+            owner_copy(0, layer, i, reduced.at[layer], pieces.at[layer, i], True).wait_recv()
+            total = total + pieces[layer, i].astype(F32)
+        total = total.astype(BF16)
+        reduced[layer] = total
+        whole[layer, pl.ds(owner, 1)] = total[None]
+        for i in range(1, owners):
+            owner_copy(1, layer, i, reduced.at[layer], whole.at[layer, owner]).start()
+
+    def unpack(layer):
+        for i in range(1, owners):
+            owner_copy(1, layer, i, reduced.at[layer], whole.at[layer, (owner + i) % owners], True).wait_recv()
+        lines = whole[layer].reshape(-1, 2 * rank).astype(F32)
+        width = dgrad.shape[1]
+        dgrad[layer] = lines[:width, :rank]
+        ugrad[layer] = lines[:width, rank:]
+        for tap in range(9):
+            start = width + tap // 2 * part
+            cgrad[layer, tap] = lines[start:start + part, tap % 2 * rank:(tap % 2 + 1) * rank]
 
     def factors(which, layer):
         own = (down, up)[which]
@@ -259,12 +315,16 @@
             cown[layer, c] = piece
             csend[layer, c] = piece.astype(BF16)
         exchange(5 + 3 * layer, lambda j: csend.at[layer, peer(j)], crecv.at[layer])
-        ugrad[layer] = nt(deltas[0], bs[layer])
+        upart[layer] = nt(deltas[0], bs[layer])
         for j in peers:
             gsend[layer, 1, j] = nt(deltas[j], bs[layer]).astype(BF16)
         exchange(6 + 3 * layer, lambda j: gsend.at[layer, 1, j], grecv.at[layer, 1])
+        if layer < LAYERS - 1:
+            scatter(layer + 1)
         finish_border(r)
         windows(r, rows, mwin)
+        if layer < LAYERS - 1:
+            gather(layer + 1)
         n = nn(kb[layer], mwin[...]).astype(BF16)
         through_factors = factors(0, layer)
         for j in (*peers, 0):
@@ -283,20 +343,20 @@
         for j in peers:
             gsend[layer, 0, j] = nt(hid[layer, j], n).astype(BF16)
         exchange(7 + 3 * layer, lambda j: gsend.at[layer, 0, j], grecv.at[layer, 0])
-        dgrad[layer] = nt(hid[layer, 0], n)
-    for layer in reversed(range(LAYERS)):
-        for k in range(3):
-            arrived(5 + 3 * layer + k)
-        total = cown[layer, pl.ds(chan, 1)][0]
-        for j in peers:
-            dgrad[layer] = dgrad[layer] + grecv[layer, 0, j].astype(F32)
-            ugrad[layer] = ugrad[layer] + grecv[layer, 1, j].astype(F32)
-            total = total + crecv[layer, j].astype(F32)
-        cgrad[layer] = total
+        dpart[layer] = nt(hid[layer, 0], n)
+    scatter(0)
     arrived(4)
     for j in peers:
         for u in range(here):
             out[pl.ds(peer(j) * here + u, 1)] = outbox[j, u][None]
+    for layer in reversed(range(1, LAYERS)):
+        unpack(layer)
+    gather(0)
+    unpack(0)
+    for layer in range(LAYERS):
+        for i in range(1, owners):
+            owner_copy(0, layer, i, packed.at[layer, (owner + i) % owners], pieces.at[layer, i]).wait_send()
+            owner_copy(1, layer, i, reduced.at[layer], whole.at[layer, owner]).wait_send()
     for copy in sent:
         copy.wait_send()
     for r in range(2 * LAYERS):
@@ -323,6 +383,8 @@
     kf = core_kernel.transpose(0, 2, 1, 3).reshape(LAYERS, rank, 9 * rank)
     kb = core_kernel[:, ::-1].transpose(0, 3, 1, 2).reshape(LAYERS, rank, 9 * rank)
     pixels = here * PIX
+    owners = tiles * subs
+    chunk = -(-(width + 5 * (rank // members)) // (16 * owners)) * 16
     vmem = pl.BlockSpec(memory_space=pltpu.VMEM)
     dma = pltpu.SemaphoreType.DMA
     out, dgrad, ugrad, cgrad = pl.pallas_call(
@@ -331,7 +393,7 @@
             jax.ShapeDtypeStruct(features.shape, BF16),
             jax.ShapeDtypeStruct((LAYERS, width, rank), F32),
             jax.ShapeDtypeStruct((LAYERS, width, rank), F32),
-            jax.ShapeDtypeStruct((LAYERS, rank // members, 9 * rank), F32),
+            jax.ShapeDtypeStruct((LAYERS, 9, rank // members, rank), F32),
         ),
         in_specs=[vmem] * 10,
         out_specs=(vmem,) * 4,
@@ -353,10 +415,18 @@
             pltpu.VMEM((LAYERS, members, rank // members, 9 * rank), BF16),
             pltpu.VMEM((LAYERS, members, rank // members, 9 * rank), BF16),
             pltpu.VMEM((LAYERS, members, rank // members, 9 * rank), F32),
+            pltpu.VMEM((LAYERS, width, rank), F32),
+            pltpu.VMEM((LAYERS, width, rank), F32),
+            pltpu.VMEM((LAYERS, owners, chunk, 2 * rank), BF16),
+            pltpu.VMEM((LAYERS, owners, chunk, 2 * rank), BF16),
+            pltpu.VMEM((LAYERS, chunk, 2 * rank), BF16),
+            pltpu.VMEM((LAYERS, owners, chunk, 2 * rank), BF16),
             dma((5 + 3 * LAYERS, members)),
             dma((5 + 3 * LAYERS, members)),
             dma((2 * LAYERS, 3 * members)),
             dma((2 * LAYERS, 3 * members)),
+            dma((2, LAYERS, owners)),
+            dma((2, LAYERS, owners)),
         ],
         compiler_params=pltpu.CompilerParams(
             collective_id=0, has_side_effects=True, vmem_limit_bytes=48 * 2**20
@@ -365,8 +435,6 @@
         features, cotangent, down_factor, up_factor, kf, kb, alive, chooser,
         jnp.asarray(border_matrix(), BF16), jnp.asarray(window_matrix(), BF16),
     )
-    dgrad, ugrad, cgrad = lax.psum((dgrad, ugrad, cgrad), ("tiles", "sub"))
-    cgrad = cgrad.reshape(LAYERS, rank // members, 9, rank).transpose(0, 2, 1, 3)
     return out, dgrad, cgrad, ugrad
 
 

time: 146 us -> 86.5 us (0.59)
  waiting for transfers between devices: 61.6 us -> 0 us
  Pallas kernels: 54.2 us -> 68 us
  between operations: 15 us -> 1.53 us
    psum x1 -> x0, waiting for transfers between devices: 61.6 us -> none  [local(): dgrad, ugrad, cgrad = lax.psum((dgrad, ugrad, cgrad), ('tiles', 'sub'))]
    pallas_call x1, Pallas kernels: 54.2 us -> 68 us  [local(): pl.pallas_call(functools.partial(kernel, (tiles, subs, members, here)), o...]
    unnamed x18 -> x22, local copies, waits for them, and re-layouts: 9.98 us -> 11.8 us
  transfers between devices with their start and end apart: 1 -> 0, of which waited for: 1 -> 0; matrix products, arithmetic and copies ran while one was open for 0% -> 0% of each run, Pallas kernels for 0% -> 0%
where the time goes in v3:
time: 86.5 us; the launch traced here: 85.9 us
  Pallas kernels  68 us (79%)
  local copies, waits for them, and re-layouts  15 us (17%)
  between operations  1.53 us (2%)
  other arithmetic  1.41 us (2%)
    pallas_call x1, Pallas kernels, local(): pl.pallas_call(functools.partial(kernel, (tiles, subs, members, here)), o...  68 us
    unnamed x22, local copies, waits for them, and re-layouts  11.8 us

profile of v3, /device:TPU:0, one launch (start us, length us, event | category | flops | bytes accessed | tf_op | source)
XLA Modules:
  0.0 85.9 jit_solution(15600416907888926801)
XLA Ops:
  0.6 0.0 copy-start
  0.6 0.0 copy-start.1
  1.5 0.7 add_select_fusion
  2.2 0.1 eq.23
  2.3 0.6 compare_convert_fusion.alive
  2.9 0.2 fusion.2
  3.1 0.1 broadcast_in_dim.40
  3.2 0.1 broadcast_in_dim.42
  3.2 0.1 broadcast_in_dim.44
  3.3 0.1 broadcast_in_dim.46
  3.4 0.1 concatenate.3
  3.5 0.1 fusion.chooser
  3.6 0.9 %copy.21.down = bf16[2,128,64]{2,1,0:T(8,128)(2,1)S(1)} copy(bf16[2,128,64]{1,2,0:T(8,128)(2,1)} %param.12) | data formatting | bytes 65536 | tf_op args[2]
  4.4 1.5 %copy.22.up = bf16[2,128,64]{2,1,0:T(8,128)(2,1)} copy(bf16[2,128,64]{1,2,0:T(8,128)(2,1)} %param.14) | data formatting | bytes 65536 | tf_op args[4]
  5.9 1.1 %copy.20 = bf16[2,64,9,64]{1,3,2,0:T(8,128)(2,1)S(1)} copy(bf16[2,64,9,64]{3,1,2,0:T(8,128)(2,1)} %bitcast.11) | data formatting | bytes 294912 | tf_op jit(solution)/shard_map/transpose | solution.py:383
  7.1 0.2 copy.23.kf
  7.3 1.0 %rev.3 = bf16[2,9,64,64]{3,2,1,0:T(8,128)(2,1)S(1)} reverse(bf16[2,9,64,64]{3,2,1,0:T(8,128)(2,1)} %param.13), dimensions={1} | reverse | bytes 294912 | tf_op jit(solution)/shard_map/rev | solution.py:384
  8.3 0.2 copy.24.kb
  8.4 0.0 copy-done
  8.5 0.0 copy-start.2
  8.5 1.0 %copy-done.2 = bf16[8,128,256]{2,1,0:T(8,128)(2,1)S(1)} copy-done((bf16[8,128,256]{2,1,0:T(8,128)(2,1)S(1)}, bf16[8,128,256]{2,1,0:T(8,128)(2,1)}, u32[]{:S(2)}) %copy-start.2) | copy-done | bytes 524312
  9.5 0.8 copy-done.3
  10.3 0.8 copy-done.6
  11.2 0.7 copy-done.7
  11.9 68.0 %shard_map.129 = (bf16[8,128,256]{2,1,0:T(8,128)(2,1)S(1)}, f32[2,128,64]{2,1,0:T(8,128)S(1)}, f32[2,128,64]{2,1,0:T(8,128)S(1)}, f32[2,9,32,64]{3,2,1,0:T(8,128)S(1)}) custom-call(bf16[8,128,256]{2,1,0:T(8,128)(2,1)S(1)} %copy-done.1, bf16[8,128,256]{2,1,0:T(8,128)(2,1)S(1)} %copy-done.2, bf16[2,128,64]{2,1,0:T(8,128)(2,1)S(1)} %copy.21.down, ...), custom_call_target="tpu_custom_call" | custom-call | tf_op jit(solution)/shard_map/pallas_call | solution.py:390
  79.9 0.0 copy-start.4
  79.9 0.6 copy-done.4
  80.5 0.7 copy-done.5
  81.2 1.6 %copy.25 = f32[2,128,64]{1,2,0:T(8,128)} copy(f32[2,128,64]{2,1,0:T(8,128)} %copy-done.5) | data formatting | bytes 131072
  82.8 1.6 %copy.26 = f32[2,128,64]{1,2,0:T(8,128)} copy(f32[2,128,64]{2,1,0:T(8,128)} %copy-done.4) | data formatting | bytes 131072
  84.4 0.8 copy.30
  85.2 0.7 copy.31
  (7 shorter events, 0.0 us)
Async XLA Ops:
  0.6 7.8 %copy-start = (bf16[384,2304]{1,0:T(8,128)(2,1)S(1)}, bf16[384,2304]{1,0:T(8,128)(2,1)}, u32[]{:S(2)}) copy-start(bf16[384,2304]{1,0:T(8,128)(2,1)} %constant.45.clone.wsel) | copy-start | bytes 5308420
  0.6 7.8 %copy-start.1 = (bf16[8,128,256]{2,1,0:T(8,128)(2,1)S(1)}, bf16[8,128,256]{2,1,0:T(8,128)(2,1)}, u32[]{:S(2)}) copy-start(bf16[8,128,256]{2,1,0:T(8,128)(2,1)} %feat.1) | copy-start | bytes 1572868
  8.5 1.0 %copy-start.2 = (bf16[8,128,256]{2,1,0:T(8,128)(2,1)S(1)}, bf16[8,128,256]{2,1,0:T(8,128)(2,1)}, u32[]{:S(2)}) copy-start(bf16[8,128,256]{2,1,0:T(8,128)(2,1)} %cot.1) | copy-start | bytes 1572868
  9.5 0.8 copy-start.3
  10.3 0.8 copy-start.6
  11.2 0.7 copy-start.7
  79.9 0.7 copy-start.4
  80.5 0.7 copy-start.5

commit v4 on v3

--- a/solution.py
+++ b/solution.py
@@ -62,7 +62,7 @@
 
 
 def kernel(
-    sizes, feat, cot, down, up, kf, kb, alive, chooser, bsel, wsel,
+    sizes, feat, cot, down, up, taps, alive, chooser, bsel, wsel,
     out, dgrad, ugrad, cgrad,
     inbox, fact, hid, grad_e, zs, bs, wins, mwin, border, ext, stage, outbox, gsend, grecv, csend, crecv, cown,
     dpart, upart, packed, pieces, reduced, whole,
@@ -73,7 +73,7 @@
     owner = lax.axis_index("tiles") * subs + lax.axis_index("sub")
     owners = tiles * subs
     has_prev, has_next = owner > 0, owner < owners - 1
-    rank = down.shape[2]
+    rank = down.shape[1]
     part = rank // members
 
     def peer(j):
@@ -164,7 +164,7 @@
     def field(factors, blocks):
         total = None
         for factor, block in zip(factors, blocks):
-            part = tn(factor, block).astype(BF16).astype(F32)
+            part = nn(factor, block).astype(BF16).astype(F32)
             total = part if total is None else total + part
         return total.astype(BF16)
 
@@ -209,7 +209,7 @@
     def rows_of(value):
         return jnp.concatenate([value[:, u * PIX:(u + 1) * PIX] for u in range(here)], axis=0)
 
-    def windows(r, rows, target):
+    def windows(r, rows, target, flipped=False):
         halos = [jnp.zeros((rank, HALO), F32) for _ in range(here)]
         for v in range(3 * members * here):
             piece = ext[r, v // (members * here), v // here % members, v % here].astype(F32)
@@ -221,7 +221,8 @@
         for tap in range(9):
             moved = nn(both, wsel[:, tap * PIX:(tap + 1) * PIX]).astype(BF16)
             for u in range(here):
-                target[tap * rank:(tap + 1) * rank, u * PIX:(u + 1) * PIX] = moved[u * rank:(u + 1) * rank]
+                to = 8 - tap if flipped else tap
+                target[to * rank:(to + 1) * rank, u * PIX:(u + 1) * PIX] = moved[u * rank:(u + 1) * rank]
 
     def scatter(layer):
         for k in range(3):
@@ -232,9 +233,11 @@
             down_sum = down_sum + grecv[layer, 0, j].astype(F32)
             up_sum = up_sum + grecv[layer, 1, j].astype(F32)
             core_sum = core_sum + crecv[layer, j].astype(F32)
-        spare = whole.shape[1] * whole.shape[2] - down_sum.shape[0] - 5 * part
+        width = down_sum.shape[1]
+        spare = whole.shape[1] * whole.shape[2] - width - 5 * part
         core_sum = jnp.concatenate([core_sum, jnp.zeros((part, rank), F32)], axis=1)
-        lines = [jnp.concatenate([down_sum, up_sum], axis=1)]
+        factor_sums = jnp.concatenate([down_sum, up_sum], axis=1)
+        lines = [factor_sums[:, k * 2 * rank:(k + 1) * 2 * rank] for k in range(width // rank)]
         lines += [core_sum[:, k * 2 * rank:(k + 1) * 2 * rank] for k in range(5)]
         if spare:
             lines.append(jnp.zeros((spare, 2 * rank), F32))
@@ -264,9 +267,10 @@
         for i in range(1, owners):
             owner_copy(1, layer, i, reduced.at[layer], whole.at[layer, (owner + i) % owners], True).wait_recv()
         lines = whole[layer].reshape(-1, 2 * rank).astype(F32)
-        width = dgrad.shape[1]
-        dgrad[layer] = lines[:width, :rank]
-        ugrad[layer] = lines[:width, rank:]
+        width = dgrad.shape[2]
+        both = jnp.concatenate([lines[k * rank:(k + 1) * rank] for k in range(width // rank)], axis=1)
+        dgrad[layer] = both[:, :width]
+        ugrad[layer] = both[:, width:]
         for tap in range(9):
             start = width + tap // 2 * part
             cgrad[layer, tap] = lines[start:start + part, tap % 2 * rank:(tap % 2 + 1) * rank]
@@ -285,7 +289,8 @@
         send_border(layer, rows)
         finish_border(layer)
         windows(layer, rows, wins.at[layer])
-        b = nn(kf[layer], wins[layer]).astype(BF16)
+        mixer = jnp.concatenate([taps[layer, tap] for tap in range(9)], axis=1)
+        b = nn(mixer, wins[layer]).astype(BF16)
         bs[layer] = b
         if layer == 0:
             arrived(2)
@@ -293,7 +298,7 @@
             for j in peers:
                 grad_e[j] = live(inbox[1, j])
         for j, factor in enumerate(factors(1, layer)):
-            z = nn(factor, b)
+            z = tn(factor, b)
             zs[layer, j] = z
             if layer < LAYERS - 1:
                 silu = z * jax.nn.sigmoid(z)
@@ -315,20 +320,20 @@
             cown[layer, c] = piece
             csend[layer, c] = piece.astype(BF16)
         exchange(5 + 3 * layer, lambda j: csend.at[layer, peer(j)], crecv.at[layer])
-        upart[layer] = nt(deltas[0], bs[layer])
+        upart[layer] = nt(bs[layer], deltas[0])
         for j in peers:
-            gsend[layer, 1, j] = nt(deltas[j], bs[layer]).astype(BF16)
+            gsend[layer, 1, j] = nt(bs[layer], deltas[j]).astype(BF16)
         exchange(6 + 3 * layer, lambda j: gsend.at[layer, 1, j], grecv.at[layer, 1])
         if layer < LAYERS - 1:
             scatter(layer + 1)
         finish_border(r)
-        windows(r, rows, mwin)
+        windows(r, rows, mwin, True)
         if layer < LAYERS - 1:
             gather(layer + 1)
-        n = nn(kb[layer], mwin[...]).astype(BF16)
+        n = tn(taps[layer].reshape(9 * rank, rank), mwin[...]).astype(BF16)
         through_factors = factors(0, layer)
         for j in (*peers, 0):
-            new_e = (grad_e[j].astype(F32) + nn(through_factors[j], n)).astype(BF16)
+            new_e = (grad_e[j].astype(F32) + tn(through_factors[j], n)).astype(BF16)
             if layer > 0:
                 grad_e[j] = new_e
                 continue
@@ -341,9 +346,9 @@
             if j == members - 1:
                 exchange(4, lambda i: stage.at[i], outbox)
         for j in peers:
-            gsend[layer, 0, j] = nt(hid[layer, j], n).astype(BF16)
+            gsend[layer, 0, j] = nt(n, hid[layer, j]).astype(BF16)
         exchange(7 + 3 * layer, lambda j: gsend.at[layer, 0, j], grecv.at[layer, 0])
-        dpart[layer] = nt(hid[layer, 0], n)
+        dpart[layer] = nt(n, hid[layer, 0])
     scatter(0)
     arrived(4)
     for j in peers:
@@ -380,8 +385,6 @@
     )
     chooser = (lane_row[:, None, :] == jnp.arange(3 * slots)[None, :, None]).astype(F32).reshape(here * 3 * slots, HALO)
     alive = (first + jnp.arange(here * PIX) // PIX < tile_count[0]).astype(F32)[None]
-    kf = core_kernel.transpose(0, 2, 1, 3).reshape(LAYERS, rank, 9 * rank)
-    kb = core_kernel[:, ::-1].transpose(0, 3, 1, 2).reshape(LAYERS, rank, 9 * rank)
     pixels = here * PIX
     owners = tiles * subs
     chunk = -(-(width + 5 * (rank // members)) // (16 * owners)) * 16
@@ -391,15 +394,15 @@
         functools.partial(kernel, (tiles, subs, members, here)),
         out_shape=(
             jax.ShapeDtypeStruct(features.shape, BF16),
-            jax.ShapeDtypeStruct((LAYERS, width, rank), F32),
-            jax.ShapeDtypeStruct((LAYERS, width, rank), F32),
+            jax.ShapeDtypeStruct((LAYERS, rank, width), F32),
+            jax.ShapeDtypeStruct((LAYERS, rank, width), F32),
             jax.ShapeDtypeStruct((LAYERS, 9, rank // members, rank), F32),
         ),
-        in_specs=[vmem] * 10,
+        in_specs=[vmem] * 9,
         out_specs=(vmem,) * 4,
         scratch_shapes=[
             pltpu.VMEM((2, members, here, width, PIX), BF16),
-            pltpu.VMEM((2, members, LAYERS, width, rank), BF16),
+            pltpu.VMEM((2, members, LAYERS, rank, width), BF16),
             pltpu.VMEM((LAYERS, members, width, pixels), BF16),
             pltpu.VMEM((members, width, pixels), BF16),
             pltpu.VMEM((LAYERS, members, width, pixels), F32),
@@ -410,13 +413,13 @@
             pltpu.VMEM((2 * LAYERS, 3, members, here, rank, HALO), BF16),
             pltpu.VMEM((members, here, width, PIX), BF16),
             pltpu.VMEM((members, here, width, PIX), BF16),
-            pltpu.VMEM((LAYERS, 2, members, width, rank), BF16),
-            pltpu.VMEM((LAYERS, 2, members, width, rank), BF16),
+            pltpu.VMEM((LAYERS, 2, members, rank, width), BF16),
+            pltpu.VMEM((LAYERS, 2, members, rank, width), BF16),
             pltpu.VMEM((LAYERS, members, rank // members, 9 * rank), BF16),
             pltpu.VMEM((LAYERS, members, rank // members, 9 * rank), BF16),
             pltpu.VMEM((LAYERS, members, rank // members, 9 * rank), F32),
-            pltpu.VMEM((LAYERS, width, rank), F32),
-            pltpu.VMEM((LAYERS, width, rank), F32),
+            pltpu.VMEM((LAYERS, rank, width), F32),
+            pltpu.VMEM((LAYERS, rank, width), F32),
             pltpu.VMEM((LAYERS, owners, chunk, 2 * rank), BF16),
             pltpu.VMEM((LAYERS, owners, chunk, 2 * rank), BF16),
             pltpu.VMEM((LAYERS, chunk, 2 * rank), BF16),
@@ -432,10 +435,10 @@
             collective_id=0, has_side_effects=True, vmem_limit_bytes=48 * 2**20
         ),
     )(
-        features, cotangent, down_factor, up_factor, kf, kb, alive, chooser,
+        features, cotangent, down_factor.transpose(0, 2, 1), up_factor.transpose(0, 2, 1), core_kernel, alive, chooser,
         jnp.asarray(border_matrix(), BF16), jnp.asarray(window_matrix(), BF16),
     )
-    return out, dgrad, cgrad, ugrad
+    return out, dgrad.transpose(0, 2, 1), cgrad, ugrad.transpose(0, 2, 1)
 
 
 def solution(mesh):

time: 86.5 us -> 79.2 us (0.916)
  local copies, waits for them, and re-layouts: 15 us -> 10.3 us
  Pallas kernels: 68 us -> 66.3 us
    unnamed x22 -> x18, local copies, waits for them, and re-layouts: 11.8 us -> 9.64 us
    pallas_call x1, Pallas kernels: 68 us -> 66.3 us  [local(): pl.pallas_call(functools.partial(kernel, (tiles, subs, members, here)), o...]
    transpose x1 -> x0, local copies, waits for them, and re-layouts: 1.15 us -> none  [local(): kf = core_kernel.transpose(0, 2, 1, 3).reshape(LAYERS, rank, 9 * rank)]
    rev x1 -> x0, local copies, waits for them, and re-layouts: 0.98 us -> none  [local(): core_kernel[:, ::-1].transpose(0, 3, 1, 2).reshape(LAYERS, rank, 9 * rank)]
where the time goes in v4:
time: 79.2 us; the launch traced here: 78.7 us
  Pallas kernels  66.3 us (84%)
  local copies, waits for them, and re-layouts  10.3 us (13%)
  between operations  1.33 us (2%)
  other arithmetic  0.81 us (1%)
    pallas_call x1, Pallas kernels, local(): pl.pallas_call(functools.partial(kernel, (tiles, subs, members, here)), o...  66.3 us
    unnamed x18, local copies, waits for them, and re-layouts  9.64 us

profile of v4, /device:TPU:0, one launch (start us, length us, event | category | flops | bytes accessed | tf_op | source)
XLA Modules:
  0.0 78.7 jit_solution(854961711947444581)
XLA Ops:
  1.3 0.7 add_select_fusion
  2.0 0.1 eq.23
  2.1 0.2 fusion.2
  2.3 0.1 broadcast_in_dim.40
  2.4 0.1 broadcast_in_dim.42
  2.5 0.1 broadcast_in_dim.44
  2.5 0.1 broadcast_in_dim.46
  2.6 0.1 concatenate.3
  2.7 0.1 fusion.chooser
  2.8 0.0 copy-start
  2.8 1.5 %copy-done = bf16[384,2304]{1,0:T(8,128)(2,1)S(1)} copy-done((bf16[384,2304]{1,0:T(8,128)(2,1)S(1)}, bf16[384,2304]{1,0:T(8,128)(2,1)}, u32[]{:S(2)}) %copy-start) | copy-done | bytes 1769496
  4.3 0.0 copy-start.1
  4.3 1.0 %copy-done.1 = bf16[8,128,256]{2,1,0:T(8,128)(2,1)S(1)} copy-done((bf16[8,128,256]{2,1,0:T(8,128)(2,1)S(1)}, bf16[8,128,256]{2,1,0:T(8,128)(2,1)}, u32[]{:S(2)}) %copy-start.1) | copy-done | bytes 524312
  5.3 0.0 copy-start.2
  5.3 1.0 %copy-done.2 = bf16[8,128,256]{2,1,0:T(8,128)(2,1)S(1)} copy-done((bf16[8,128,256]{2,1,0:T(8,128)(2,1)S(1)}, bf16[8,128,256]{2,1,0:T(8,128)(2,1)}, u32[]{:S(2)}) %copy-start.2) | copy-done | bytes 524312
  6.4 0.0 copy-start.3
  6.4 1.0 %copy-done.3 = bf16[2,9,64,64]{3,2,1,0:T(8,128)(2,1)S(1)} copy-done((bf16[2,9,64,64]{3,2,1,0:T(8,128)(2,1)S(1)}, bf16[2,9,64,64]{3,2,1,0:T(8,128)(2,1)}, u32[]{:S(2)}) %copy-start.3) | copy-done | bytes 147480
  7.3 0.0 copy-start.4
  7.3 0.8 %copy-done.4 = bf16[256,128]{1,0:T(8,128)(2,1)S(1)} copy-done((bf16[256,128]{1,0:T(8,128)(2,1)S(1)}, bf16[256,128]{1,0:T(8,128)(2,1)}, u32[]{:S(2)}) %copy-start.4) | copy-done | bytes 65560
  8.2 0.0 copy-start.5
  8.2 0.8 copy-done.5
  8.9 0.0 copy-start.6
  8.9 0.8 copy-done.6
  9.7 66.3 %shard_map.129 = (bf16[8,128,256]{2,1,0:T(8,128)(2,1)S(1)}, f32[2,64,128]{2,1,0:T(8,128)S(1)}, f32[2,64,128]{2,1,0:T(8,128)S(1)}, f32[2,9,32,64]{3,2,1,0:T(8,128)S(1)}) custom-call(bf16[8,128,256]{2,1,0:T(8,128)(2,1)S(1)} %copy-done.1, bf16[8,128,256]{2,1,0:T(8,128)(2,1)S(1)} %copy-done.2, bf16[2,64,128]{2,1,0:T(8,128)(2,1)S(1)} %bitcast.12, ...), custom_call_target="tpu_custom_call" | custom-call | tf_op jit(solution)/shard_map/pallas_call | solution.py:393
  76.0 0.8 %copy.19 = bf16[8,128,256]{2,1,0:T(8,128)(2,1)} copy(bf16[8,128,256]{2,1,0:T(8,128)(2,1)S(1)} %get-tuple-element.28) | data formatting | bytes 1048576
  76.8 0.6 copy.20
  77.4 0.7 copy.21
  78.1 0.6 copy.22
  (3 shorter events, 0.0 us)
Async XLA Ops:
  2.8 1.5 %copy-start = (bf16[384,2304]{1,0:T(8,128)(2,1)S(1)}, bf16[384,2304]{1,0:T(8,128)(2,1)}, u32[]{:S(2)}) copy-start(bf16[384,2304]{1,0:T(8,128)(2,1)} %constant.45.clone.wsel) | copy-start | bytes 5308420
  4.3 1.0 %copy-start.1 = (bf16[8,128,256]{2,1,0:T(8,128)(2,1)S(1)}, bf16[8,128,256]{2,1,0:T(8,128)(2,1)}, u32[]{:S(2)}) copy-start(bf16[8,128,256]{2,1,0:T(8,128)(2,1)} %feat.1) | copy-start | bytes 1572868
  5.3 1.0 %copy-start.2 = (bf16[8,128,256]{2,1,0:T(8,128)(2,1)S(1)}, bf16[8,128,256]{2,1,0:T(8,128)(2,1)}, u32[]{:S(2)}) copy-start(bf16[8,128,256]{2,1,0:T(8,128)(2,1)} %cot.1) | copy-start | bytes 1572868
  6.4 1.0 %copy-start.3 = (bf16[2,9,64,64]{3,2,1,0:T(8,128)(2,1)S(1)}, bf16[2,9,64,64]{3,2,1,0:T(8,128)(2,1)}, u32[]{:S(2)}) copy-start(bf16[2,9,64,64]{3,2,1,0:T(8,128)(2,1)} %taps.1) | copy-start | bytes 442372
  7.3 0.8 %copy-start.4 = (bf16[256,128]{1,0:T(8,128)(2,1)S(1)}, bf16[256,128]{1,0:T(8,128)(2,1)}, u32[]{:S(2)}) copy-start(bf16[256,128]{1,0:T(8,128)(2,1)} %constant.44.clone.bsel) | copy-start | bytes 196612
  8.2 0.8 copy-start.5
  8.9 0.8 copy-start.6

commit v5 on v4

--- a/solution.py
+++ b/solution.py
@@ -62,11 +62,11 @@
 
 
 def kernel(
-    sizes, feat, cot, down, up, taps, alive, chooser, bsel, wsel,
+    sizes, feat, cot, down, up, taps, alive, chooser, bsel, wsel_far,
     out, dgrad, ugrad, cgrad,
     inbox, fact, hid, grad_e, zs, bs, wins, mwin, border, ext, stage, outbox, gsend, grecv, csend, crecv, cown,
     dpart, upart, packed, pieces, reduced, whole,
-    send_sem, recv_sem, bsend_sem, brecv_sem, rsend_sem, rrecv_sem,
+    send_sem, recv_sem, bsend_sem, brecv_sem, rsend_sem, rrecv_sem, wsel, local_sem,
 ):
     tiles, subs, members, here = sizes
     chan = lax.axis_index("chan")
@@ -98,6 +98,17 @@
             action()
         else:
             pl.when(cond)(action)
+
+    def slots_of(j):
+        return pl.ds(peer(j) * here, here)
+
+    own_copies = [
+        pltpu.make_async_copy(feat.at[slots_of(0)], inbox.at[0, 0], local_sem.at[0]),
+        pltpu.make_async_copy(cot.at[slots_of(0)], inbox.at[1, 0], local_sem.at[1]),
+        pltpu.make_async_copy(wsel_far, wsel, local_sem.at[2]),
+    ]
+    for copy in own_copies:
+        copy.start()
 
     @pl.when(jnp.logical_not(has_prev))
     def _():
@@ -131,9 +142,6 @@
             device_id={"chan": peer(j)}, device_id_type=MESH,
         )
 
-    def slots_of(j):
-        return pl.ds(peer(j) * here, here)
-
     peers = range(1, members)
     sent, arrivals = [], {}
 
@@ -158,8 +166,10 @@
     def live(x):
         return (lanes(x).astype(F32) * alive[...]).astype(BF16)
 
-    hid[0, 0] = live(feat[slots_of(0)])
-    grad_e[0] = live(cot[slots_of(0)])
+    for copy in own_copies:
+        copy.wait()
+    hid[0, 0] = live(inbox[0, 0])
+    grad_e[0] = live(inbox[1, 0])
 
     def field(factors, blocks):
         total = None
@@ -389,6 +399,7 @@
     owners = tiles * subs
     chunk = -(-(width + 5 * (rank // members)) // (16 * owners)) * 16
     vmem = pl.BlockSpec(memory_space=pltpu.VMEM)
+    far = pl.BlockSpec(memory_space=pltpu.HBM)
     dma = pltpu.SemaphoreType.DMA
     out, dgrad, ugrad, cgrad = pl.pallas_call(
         functools.partial(kernel, (tiles, subs, members, here)),
@@ -398,7 +409,7 @@
             jax.ShapeDtypeStruct((LAYERS, rank, width), F32),
             jax.ShapeDtypeStruct((LAYERS, 9, rank // members, rank), F32),
         ),
-        in_specs=[vmem] * 9,
+        in_specs=[far, far] + [vmem] * 6 + [far],
         out_specs=(vmem,) * 4,
         scratch_shapes=[
             pltpu.VMEM((2, members, here, width, PIX), BF16),
@@ -430,6 +441,8 @@
             dma((2 * LAYERS, 3 * members)),
             dma((2, LAYERS, owners)),
             dma((2, LAYERS, owners)),
+            pltpu.VMEM((PIX + HALO, 9 * PIX), BF16),
+            dma((3,)),
         ],
         compiler_params=pltpu.CompilerParams(
             collective_id=0, has_side_effects=True, vmem_limit_bytes=48 * 2**20

time: 79.2 us -> 79.7 us (level)
  no operation moved by 1% of the time
where the time goes in v5:
time: 79.7 us; the launch traced here: 79.2 us
  Pallas kernels  66.7 us (84%)
  local copies, waits for them, and re-layouts  10.3 us (13%)
  between operations  1.33 us (2%)
  other arithmetic  0.81 us (1%)
    pallas_call x1, Pallas kernels, local(): pl.pallas_call(functools.partial(kernel, (tiles, subs, members, here)), o...  66.7 us
    unnamed x18, local copies, waits for them, and re-layouts  9.64 us

profile of v5, /device:TPU:0, one launch (start us, length us, event | category | flops | bytes accessed | tf_op | source)
XLA Modules:
  0.0 79.2 jit_solution(231914093193292743)
XLA Ops:
  1.3 0.7 add_select_fusion
  2.0 0.1 eq.23
  2.1 0.2 fusion.2
  2.3 0.1 broadcast_in_dim.40
  2.4 0.1 broadcast_in_dim.42
  2.5 0.1 broadcast_in_dim.44
  2.5 0.1 broadcast_in_dim.46
  2.6 0.1 concatenate.3
  2.7 0.1 fusion.chooser
  2.8 0.0 copy-start
  2.8 1.5 %copy-done = bf16[384,2304]{1,0:T(8,128)(2,1)S(1)} copy-done((bf16[384,2304]{1,0:T(8,128)(2,1)S(1)}, bf16[384,2304]{1,0:T(8,128)(2,1)}, u32[]{:S(2)}) %copy-start) | copy-done | bytes 1769496
  4.3 0.0 copy-start.1
  4.3 1.0 %copy-done.1 = bf16[8,128,256]{2,1,0:T(8,128)(2,1)S(1)} copy-done((bf16[8,128,256]{2,1,0:T(8,128)(2,1)S(1)}, bf16[8,128,256]{2,1,0:T(8,128)(2,1)}, u32[]{:S(2)}) %copy-start.1) | copy-done | bytes 524312
  5.3 0.0 copy-start.2
  5.3 1.0 %copy-done.2 = bf16[8,128,256]{2,1,0:T(8,128)(2,1)S(1)} copy-done((bf16[8,128,256]{2,1,0:T(8,128)(2,1)S(1)}, bf16[8,128,256]{2,1,0:T(8,128)(2,1)}, u32[]{:S(2)}) %copy-start.2) | copy-done | bytes 524312
  6.4 0.0 copy-start.3
  6.4 1.0 %copy-done.3 = bf16[2,9,64,64]{3,2,1,0:T(8,128)(2,1)S(1)} copy-done((bf16[2,9,64,64]{3,2,1,0:T(8,128)(2,1)S(1)}, bf16[2,9,64,64]{3,2,1,0:T(8,128)(2,1)}, u32[]{:S(2)}) %copy-start.3) | copy-done | bytes 147480
  7.3 0.0 copy-start.4
  7.3 0.8 %copy-done.4 = bf16[256,128]{1,0:T(8,128)(2,1)S(1)} copy-done((bf16[256,128]{1,0:T(8,128)(2,1)S(1)}, bf16[256,128]{1,0:T(8,128)(2,1)}, u32[]{:S(2)}) %copy-start.4) | copy-done | bytes 65560
  8.2 0.0 copy-start.5
  8.2 0.8 copy-done.5
  8.9 0.0 copy-start.6
  8.9 0.8 copy-done.6
  9.7 66.7 %shard_map.129 = (bf16[8,128,256]{2,1,0:T(8,128)(2,1)S(1)}, f32[2,64,128]{2,1,0:T(8,128)S(1)}, f32[2,64,128]{2,1,0:T(8,128)S(1)}, f32[2,9,32,64]{3,2,1,0:T(8,128)S(1)}) custom-call(bf16[8,128,256]{2,1,0:T(8,128)(2,1)S(1)} %copy-done.1, bf16[8,128,256]{2,1,0:T(8,128)(2,1)S(1)} %copy-done.2, bf16[2,64,128]{2,1,0:T(8,128)(2,1)S(1)} %bitcast.12, ...), custom_call_target="tpu_custom_call" | custom-call | tf_op jit(solution)/shard_map/pallas_call | solution.py:404
  76.4 0.8 %copy.19 = bf16[8,128,256]{2,1,0:T(8,128)(2,1)} copy(bf16[8,128,256]{2,1,0:T(8,128)(2,1)S(1)} %get-tuple-element.28) | data formatting | bytes 1048576
  77.2 0.6 copy.20
  77.8 0.7 copy.21
  78.5 0.6 copy.22
  (3 shorter events, 0.0 us)
Async XLA Ops:
  2.8 1.5 %copy-start = (bf16[384,2304]{1,0:T(8,128)(2,1)S(1)}, bf16[384,2304]{1,0:T(8,128)(2,1)}, u32[]{:S(2)}) copy-start(bf16[384,2304]{1,0:T(8,128)(2,1)} %constant.45.clone.wsel_far) | copy-start | bytes 5308420
  4.3 1.0 %copy-start.1 = (bf16[8,128,256]{2,1,0:T(8,128)(2,1)S(1)}, bf16[8,128,256]{2,1,0:T(8,128)(2,1)}, u32[]{:S(2)}) copy-start(bf16[8,128,256]{2,1,0:T(8,128)(2,1)} %feat.1) | copy-start | bytes 1572868
  5.3 1.0 %copy-start.2 = (bf16[8,128,256]{2,1,0:T(8,128)(2,1)S(1)}, bf16[8,128,256]{2,1,0:T(8,128)(2,1)}, u32[]{:S(2)}) copy-start(bf16[8,128,256]{2,1,0:T(8,128)(2,1)} %cot.1) | copy-start | bytes 1572868
  6.4 1.0 %copy-start.3 = (bf16[2,9,64,64]{3,2,1,0:T(8,128)(2,1)S(1)}, bf16[2,9,64,64]{3,2,1,0:T(8,128)(2,1)}, u32[]{:S(2)}) copy-start(bf16[2,9,64,64]{3,2,1,0:T(8,128)(2,1)} %taps.1) | copy-start | bytes 442372
  7.3 0.8 %copy-start.4 = (bf16[256,128]{1,0:T(8,128)(2,1)S(1)}, bf16[256,128]{1,0:T(8,128)(2,1)}, u32[]{:S(2)}) copy-start(bf16[256,128]{1,0:T(8,128)(2,1)} %constant.44.clone.bsel) | copy-start | bytes 196612
  8.2 0.8 copy-start.5
  8.9 0.8 copy-start.6
